TPU v7x, 256 devices: a whole 4x4x8 slice. The times are simulated.
256 devices in a mesh: wave: 128 (over x, y, z), lev: 2 (over core).
Axes of the slice: x: 4, y: 4, z: 8, core: 2. Of those that a mesh axis runs over, the one named last changes fastest.
Arguments:
- spectra: bfloat16 [1280, 192, 1280], P('wave', 'lev'), may hold values from -0.19921875 to 0.19921875
- legendre: bfloat16 [1280, 128, 1280], P('wave'), may hold values from -0.15625 to 0.15625
- wave_slots: int32 [1280], replicated, may hold values from 0 to 1279, as said below
- row_length: int32 [256], P('wave'), may hold values from 20 to 5136, as said below
Outputs:
- grid_out: bfloat16 [256, 96, 5136], P('wave', None, 'lev')
Inputs may be any that keep to these rules, and one draw needn't show every extreme that they name: `wave_slots`: a permutation of 0 to 1279 in which slots 2k and 2k+1 hold m and 1279 - m. Each value is 20 plus four times a whole number below 1280; row_length[128 + i] equals row_length[i].
All inputs are finite; a program needn't handle non-finite values.
Results may differ from a plain program's by a relative error of at most 0.0061.
Values may be sent and summed in bfloat16 or wider, within the bound.
No kernel may reach another device: no remote copies, remote signals or barrier semaphores. Data moves between devices by JAX's collectives and lax.ppermute only.
A program may use at most 256 MiB of HBM per device.

v0:
```python
import jax
import jax.numpy as jnp
from jax import lax
from jax.sharding import PartitionSpec as P


def twiddles(wave_list, length, starts):
    phases = wave_list[:, None] * starts[None, :] % length
    angles = 2.0 * jnp.pi * phases.astype(jnp.float32) / length.astype(jnp.float32)
    return (jnp.cos(angles), jnp.sin(angles))


def half_row(band_real, band_imag, wave_list, length, side, half_width):
    count = -(-half_width // 512)
    starts = side * half_width + 512 * jnp.arange(count, dtype=jnp.int32)
    cos_a, sin_a = twiddles(wave_list, length, starts)
    cos_b, sin_b = twiddles(wave_list, length, jnp.arange(512, dtype=jnp.int32))
    weights = jnp.where(wave_list == 0, 1.0, 2.0).astype(jnp.float32)
    weights = jnp.where(wave_list <= (length - 1) // 2, weights, 0.0)
    real_part = band_real.astype(jnp.float32) * weights[:, None]
    imag_part = band_imag.astype(jnp.float32) * weights[:, None]
    turned_real = (
        real_part[:, None, :] * cos_a[:, :, None] - imag_part[:, None, :] * sin_a[:, :, None]
    ).astype(jnp.bfloat16)
    turned_imag = (
        real_part[:, None, :] * sin_a[:, :, None] + imag_part[:, None, :] * cos_a[:, :, None]
    ).astype(jnp.bfloat16)
    offset_cos = cos_b.astype(jnp.bfloat16)
    offset_sin = (-sin_b).astype(jnp.bfloat16)
    values = jnp.einsum("mak,mb->kab", turned_real, offset_cos, preferred_element_type=jnp.float32)
    values = values + jnp.einsum(
        "mak,mb->kab", turned_imag, offset_sin, preferred_element_type=jnp.float32
    )
    values = values.reshape(values.shape[0], count * 512)[:, :half_width]
    columns = side * half_width + jnp.arange(half_width, dtype=jnp.int32)
    return jnp.where(columns[None, :] < length, values, 0.0)


def fourier_rows(arrived, lengths, wave_list, sides, half_width):
    results = []
    for latitude in range(arrived.shape[1]):
        band_real = arrived[:, latitude, 0]
        band_imag = arrived[:, latitude, 1]
        pieces = [
            half_row(band_real, band_imag, wave_list, lengths[latitude], side, half_width)
            for side in sides
        ]
        results.append(jnp.concatenate(pieces, axis=1).astype(jnp.bfloat16))
    return jnp.stack(results)


def on_device(spectra, legendre, wave_slots, row_length):
    slot_count = spectra.shape[0]
    degrees = spectra.shape[2]
    fields = spectra.shape[1] // 2
    total_m = wave_slots.shape[0]
    lon_total = 4 * total_m + 16
    half_width = lon_total // 2
    wave_place = lax.axis_index("wave")
    own_waves = lax.dynamic_slice_in_dim(wave_slots, wave_place * slot_count, slot_count)
    degree = lax.broadcasted_iota(jnp.int32, (slot_count, degrees), 1)
    kept_mask = (degree >= (own_waves // 64 * 64)[:, None]).astype(jnp.bfloat16)
    spectrum = spectra.reshape(slot_count, fields, 2, degrees) * kept_mask[:, None, None, :]
    parity_signs = (1 - 2 * ((degree - own_waves[:, None]) % 2)).astype(jnp.bfloat16)
    signed_spectrum = spectrum * parity_signs[:, None, None, :]
    north_values = jnp.einsum(
        "sln,sqrn->slrq", legendre, spectrum, preferred_element_type=jnp.float32
    )
    south_values = jnp.einsum(
        "sln,sqrn->slrq", legendre, signed_spectrum, preferred_element_type=jnp.float32
    )
    band_values = jnp.concatenate(
        [north_values.astype(jnp.bfloat16), south_values.astype(jnp.bfloat16)], axis=1
    )
    grid_local = fourier_rows(
        lax.all_to_all(band_values, "wave", split_axis=1, concat_axis=0, tiled=True),
        row_length,
        wave_slots,
        (0, 1),
        half_width,
    )
    return lax.all_to_all(grid_local, "lev", split_axis=2, concat_axis=1, tiled=True)


def solution(mesh):
    placed = (P("wave", "lev", None), P("wave", None, None), P(), P("wave"))
    return jax.shard_map(
        on_device, mesh=mesh, in_specs=placed, out_specs=P("wave", None, "lev"), check_vma=False
    )
```

profile of v0, /device:TPU:1, one launch (start us, length us, event | category | flops | bytes accessed | tf_op | source)
XLA Modules:
  0.0 398.5 jit_solution(12508951524492504462)
XLA Ops:
  0.0 0.0 copy-start
  0.0 0.9 fusion.103
  0.9 0.1 fusion.64
  1.0 0.1 fusion.60
  1.1 6.1 %reshape.472 = bf16[10,48,2,1280]{3,2,1,0:T(2,128)(2,1)} reshape(bf16[10,96,1280]{2,1,0:T(8,128)(2,1)} %param.4) | data formatting | bytes 4915200 | tf_op jit(solution)/shard_map/reshape | solution.py:63
  7.3 0.0 copy-done
  7.3 0.0 copy-start.1
  7.3 3.0 fusion.45
  10.3 0.0 copy-done.1
  10.3 1.2 fusion.40
  11.4 0.0 copy-start.3
  11.5 0.8 pad_maximum_fusion.2
  12.3 0.0 copy-start.2
  12.3 3.7 copy.34
  16.0 4.9 %reshape.498 = bf16[128,2,960]{2,1,0:T(2,128)(2,1)} reshape(bf16[256,10,2,48]{3,2,1,0:T(2,128)(2,1)} %bitcast.97) | data formatting | bytes 983040
  20.9 17.1 %all-to-all-start = ((bf16[128,2,960]{2,1,0:T(2,128)(2,1)}), bf16[128,2,960]{2,1,0:T(2,128)(2,1)}, u32[]{:S(2)}, u32[]{:S(2)}) async-start(bf16[128,2,960]{2,1,0:T(2,128)(2,1)} %reshape.498), calls=%async_computation | async-start | bytes 1048576 | tf_op jit(solution)/shard_map/all_to_all | solution.py:76
  38.0 0.0 copy-done.3
  38.0 0.6 fusion.121
  43.7 0.6 fusion.102
  44.3 0.6 iota_compare_fusion.1
  45.0 0.0 copy-done.2
  45.0 2.9 fusion.100
  47.9 8.7 %all-to-all-done = bf16[128,2,960]{2,1,0:T(2,128)(2,1)} async-done(((bf16[128,2,960]{2,1,0:T(2,128)(2,1)}), bf16[128,2,960]{2,1,0:T(2,128)(2,1)}, u32[]{:S(2)}, u32[]{:S(2)}) %all-to-all-start) | async-done | bytes 491552 | tf_op jit(solution)/shard_map/all_to_all | solution.py:76
  56.7 5.2 %reshape.499 = bf16[256,10,2,48]{3,2,1,0:T(2,128)(2,1)} reshape(bf16[128,2,960]{2,1,0:T(2,128)(2,1)} %all-to-all-done) | data formatting | bytes 983040
  61.8 1.6 copy.35
  63.4 2.0 copy.36
  65.4 3.1 fusion.120
  68.5 1.3 convert_multiply_fusion.1
  69.8 1.3 copy.38
  71.1 2.0 copy.39
  73.1 2.6 convert_multiply_fusion
  75.7 2.0 copy.43
  77.7 2.0 copy.44
  79.7 3.1 add_convert_fusion.1
  82.8 34.8 %fusion.25 = f32[512,288]{0,1:S(1)} fusion(bf16[1280,288]{0,1:T(8,128)(2,1)S(1)} %bitcast.113, f32[]{:T(128)S(6)} %convert_element_type.187, pred[]{:T(512)S(6)} %lt.116, s32[]{:T(128)S(6)} %select_n.121, s32[1280]{0:T(1024)S(1)} %copy-done.2), kind=kOutput, calls=%fused_computation.41 | convolution fusion | flops 385351680 | bytes 1332233
  117.6 35.0 %fusion.27 = f32[512,288]{0,1:S(1)} fusion(bf16[1280,288]{0,1:T(8,128)(2,1)S(1)} %bitcast.112, f32[]{:T(128)S(6)} %convert_element_type.187, pred[]{:T(512)S(6)} %lt.116, s32[]{:T(128)S(6)} %select_n.121, s32[1280]{0:T(1024)S(1)} %copy-done.2), kind=kOutput, calls=%fused_computation.43 | convolution fusion | flops 386007040 | bytes 1332233
  152.6 0.1 add_bitcast_fusion.3
  152.8 34.8 %fusion.26 = f32[512,288]{0,1:S(1)} fusion(bf16[1280,288]{0,1:T(8,128)(2,1)S(1)} %bitcast.111, f32[]{:T(128)S(6)} %convert_element_type.187, pred[]{:T(512)S(6)} %lt.116, s32[]{:T(128)S(6)} %select_n.121, s32[1280]{0:T(1024)S(1)} %copy-done.2), kind=kOutput, calls=%fused_computation.42 | convolution fusion | flops 385351680 | bytes 1332233
  187.6 35.0 %fusion.28 = f32[512,288]{0,1:S(1)} fusion(bf16[1280,288]{0,1:T(8,128)(2,1)S(1)} %bitcast.110, f32[]{:T(128)S(6)} %convert_element_type.187, pred[]{:T(512)S(6)} %lt.116, s32[]{:T(128)S(6)} %select_n.121, s32[1280]{0:T(1024)S(1)} %copy-done.2), kind=kOutput, calls=%fused_computation.44 | convolution fusion | flops 386007040 | bytes 1332233
  222.6 0.1 add_bitcast_fusion.2
  222.7 34.8 %fusion.21 = f32[512,288]{0,1:S(1)} fusion(bf16[1280,288]{0,1:T(8,128)(2,1)S(1)} %bitcast.109, f32[]{:T(128)S(6)} %convert_element_type.207, pred[]{:T(512)S(6)} %lt.125, s32[]{:T(128)S(6)} %select_n.133, s32[1280]{0:T(1024)S(1)} %copy-done.2), kind=kOutput, calls=%fused_computation.37 | convolution fusion | flops 385351680 | bytes 1332233
  257.6 35.0 %fusion.23 = f32[512,288]{0,1:S(1)} fusion(bf16[1280,288]{0,1:T(8,128)(2,1)S(1)} %bitcast.108, f32[]{:T(128)S(6)} %convert_element_type.207, pred[]{:T(512)S(6)} %lt.125, s32[]{:T(128)S(6)} %select_n.133, s32[1280]{0:T(1024)S(1)} %copy-done.2), kind=kOutput, calls=%fused_computation.39 | convolution fusion | flops 386007040 | bytes 1332233
  292.5 0.1 add_bitcast_fusion.1
  292.7 35.0 %fusion.24 = f32[512,288]{0,1:S(1)} fusion(bf16[1280,288]{0,1:T(8,128)(2,1)S(1)} %bitcast.107, f32[]{:T(128)S(6)} %convert_element_type.207, pred[]{:T(512)S(6)} %lt.125, s32[]{:T(128)S(6)} %select_n.133, s32[1280]{0:T(1024)S(1)} %copy-done.2), kind=kOutput, calls=%fused_computation.40 | convolution fusion | flops 386007040 | bytes 1332233
  327.7 34.7 %fusion.22 = f32[512,288]{0,1:S(1)} fusion(bf16[1280,288]{0,1:T(8,128)(2,1)S(1)} %bitcast.106, f32[]{:T(128)S(6)} %convert_element_type.207, pred[]{:T(512)S(6)} %lt.125, s32[]{:T(128)S(6)} %select_n.133, s32[1280]{0:T(1024)S(1)} %copy-done.2), kind=kOutput, calls=%fused_computation.38 | convolution fusion | flops 385351680 | bytes 1332233
  362.4 0.1 add_bitcast_fusion
  362.5 0.1 fusion.53
  362.6 0.1 fusion.54
  362.6 0.1 fusion.55
  362.7 0.1 fusion.56
  362.7 1.2 fusion.48
  363.9 6.5 %copy.47 = bf16[2,48,5136]{1,0,2:T(2,128)(2,1)} copy(bf16[2,48,5136]{2,1,0:T(8,128)(2,1)} %fusion.48) | data formatting | bytes 1972224 | tf_op jit(solution)/shard_map/stack | solution.py:49
  370.5 6.3 %reshape.500 = bf16[2,2,123264]{2,1,0:T(2,128)(2,1)} reshape(bf16[5136,2,48]{2,1,0:T(2,128)(2,1)} %bitcast.95) | data formatting | bytes 1972224
  376.8 8.7 %all_to_all.36 = bf16[2,2,123264]{2,1,0:T(2,128)(2,1)} all-to-all(bf16[2,2,123264]{2,1,0:T(2,128)(2,1)} %reshape.500), channel_id=1, replica_groups=mesh['wave'=128,'lev'=2] {'lev'}, dimensions={0} | all-to-all | bytes 1972224 | tf_op jit(solution)/shard_map/all_to_all | solution.py:82
  385.5 5.6 %reshape.501 = bf16[5136,2,48]{2,1,0:T(2,128)(2,1)} reshape(bf16[2,2,123264]{2,1,0:T(2,128)(2,1)} %all_to_all.36) | data formatting | bytes 1972224
  391.1 6.9 %copy.49 = bf16[2,2,48,2568]{3,2,1,0:T(8,128)(2,1)} copy(bf16[2,2,48,2568]{2,0,3,1:T(2,128)(2,1)} %bitcast.96) | data formatting | bytes 1972224 | tf_op jit(solution)/shard_map/all_to_all | solution.py:82
  (7 shorter events, 0.1 us)
Async XLA Ops:
  0.0 7.3 %copy-start = (bf16[10,128,1280]{2,1,0:T(8,128)(2,1)S(1)}, bf16[10,128,1280]{2,1,0:T(8,128)(2,1)}, u32[]{:S(2)}) copy-start(bf16[10,128,1280]{2,1,0:T(8,128)(2,1)} %param.5) | copy-start | bytes 9830404
  7.3 3.0 copy-start.1
  11.4 26.5 %copy-start.3 = (s32[2]{0:T(128)S(1)}, s32[2]{0:T(128)}, u32[]{:S(2)}) copy-start(s32[2]{0:T(128)} %param.7) | copy-start | bytes 28
  12.3 32.7 %copy-start.2 = (s32[1280]{0:T(1024)S(1)}, s32[1280]{0:T(1024)}, u32[]{:S(2)}) copy-start(s32[1280]{0:T(1024)} %param.6) | copy-start | bytes 15364
  20.9 35.8 %all-to-all-start = ((bf16[128,2,960]{2,1,0:T(2,128)(2,1)}), bf16[128,2,960]{2,1,0:T(2,128)(2,1)}, u32[]{:S(2)}, u32[]{:S(2)}) async-start(bf16[128,2,960]{2,1,0:T(2,128)(2,1)} %reshape.498), calls=%async_computation | async-start | bytes 1048576 | tf_op jit(solution)/shard_map/all_to_all | solution.py:76
where the time goes:
time: 406 us; the launch traced here: 399 us
  matrix products  283 us (70%)
  local copies, waits for them, and re-layouts  56.9 us (14%)
  other arithmetic  18.1 us (4%)
  starting transfers between devices  17.1 us (4%)
  waiting for transfers between devices  8.71 us (2%)
  blocking collectives  8.68 us (2%)
  between operations  5.78 us (1%)
    unnamed x8, matrix products  279 us
    unnamed x12, local copies, waits for them, and re-layouts  22.1 us
    all_to_all x1, starting transfers between devices, on_device(): lax.all_to_all(band_values, 'wave', split_axis=1, concat_axis=0, tiled=True)  17.1 us
    all_to_all x1, waiting for transfers between devices, on_device(): lax.all_to_all(band_values, 'wave', split_axis=1, concat_axis=0, tiled=True)  8.71 us
    all_to_all x1, blocking collectives, on_device(): lax.all_to_all(grid_local, 'lev', split_axis=2, concat_axis=1, tiled=True)  8.68 us
  transfers between devices with their start and end apart: 1, of which 1 were waited for; matrix products, arithmetic and copies ran while one was open for 1% of the time, Pallas kernels for 0%

commit v1 on v0

v1 whole, which is shorter than its diff:
```python
import functools
import math

import jax
import jax.numpy as jnp
from jax import lax
from jax.experimental import pallas as pl
from jax.experimental.pallas import tpu as pltpu
from jax.sharding import PartitionSpec as P

BLOCK = 512
NT = (((1,), (1,)), ((), ()))
CHUNK = 256


def legendre_kernel(waves, first, legendre, spectra, sent, tables, spectrum, product, rows, sems):
    slots, columns, degrees = spectrum.shape
    chunks = degrees // CHUNK

    def each(slot, act):
        chunk = waves[first[0] + slot] // CHUNK
        for number in range(chunks):
            kept = pl.ds(number * CHUNK, degrees - number * CHUNK)

            @pl.when(chunk == number)
            def _():
                act(
                    kept,
                    pltpu.make_async_copy(
                        legendre.at[slot, :, kept], tables.at[slot, :, kept], sems.at[slot, 0]
                    ),
                    pltpu.make_async_copy(
                        spectra.at[slot, :, kept], spectrum.at[slot, :, kept], sems.at[slot, 1]
                    ),
                )

    def begin(kept, one, two):
        one.start()
        two.start()

    @pl.loop(0, slots)
    def _(slot):
        each(slot, begin)

    for hemisphere in (0, 1):
        for lat in (0, 1):
            rows[pl.ds(hemisphere * 1024 + lat * 8, 64, stride=16), :] = jnp.zeros(
                (64, 128), jnp.float32
            )
    lane = lax.broadcasted_iota(jnp.int32, (64, 128), 1)
    blank = 128 - columns

    @pl.loop(0, slots)
    def _(slot):
        wave = waves[first[0] + slot]

        def sums(kept, one, two):
            one.wait()
            two.wait()
            degree = lax.broadcasted_iota(jnp.int32, (1, kept.size), 1) + kept.start
            mask = jnp.where(degree >= wave // 64 * 64, 1.0, 0.0)
            signed = jnp.where((degree - wave) % 2 == 0, mask, -mask).astype(jnp.bfloat16)
            mask = mask.astype(jnp.bfloat16)
            own = spectrum[slot, :, kept]
            zero = jnp.zeros((blank, kept.size), jnp.bfloat16)
            both = lax.dot_general(
                tables[slot, :, kept],
                jnp.concatenate([own * mask, zero, own * signed, zero], axis=0),
                NT,
                preferred_element_type=jnp.float32,
            )
            product[0:128] = both[:, 0:128]
            product[128:256] = both[:, 128:256]

        each(slot, sums)
        place = slot * columns // 128
        shift = slot * columns % 128
        for hemisphere in (0, 1):
            for lat in (0, 1):
                band = pltpu.roll(product[pl.ds(hemisphere * 128 + lat, 64, stride=2), :], shift, 1)
                base = hemisphere * 1024 + lat * 8 + place
                here, after = pl.ds(base, 64, stride=16), pl.ds(base + 1, 64, stride=16)
                rows[here, :] = jnp.where(lane >= shift, band, rows[here, :])
                rows[after, :] = jnp.where(lane < shift, band, 0.0)

    sent[...] = rows[...].astype(jnp.bfloat16).reshape(sent.shape)


def legendre_call(waves, first, legendre, spectra):
    slots, lats, degrees = legendre.shape
    columns = spectra.shape[1]
    return pl.pallas_call(
        legendre_kernel,
        out_shape=jax.ShapeDtypeStruct((128, 16, 128), jnp.bfloat16),
        in_specs=[pl.BlockSpec(memory_space=pltpu.SMEM)] * 2 + [pl.BlockSpec(memory_space=pl.ANY)] * 2,
        out_specs=pl.BlockSpec(memory_space=pltpu.VMEM),
        scratch_shapes=[
            pltpu.VMEM((slots, lats, degrees), jnp.bfloat16),
            pltpu.VMEM((slots, columns, degrees), jnp.bfloat16),
            pltpu.VMEM((2 * lats, 128), jnp.float32),
            pltpu.VMEM((2048, 128), jnp.float32),
            pltpu.SemaphoreType.DMA((slots, 2)),
        ],
        compiler_params=pltpu.CompilerParams(vmem_limit_bytes=60 << 20),
        name="legendre",
    )(waves, first, legendre, spectra)


def circle(waves, starts, length):
    whole = waves * starts
    turns = jnp.floor(whole * (1.0 / length))
    phase = whole - turns * length
    phase = jnp.where(phase < 0.0, phase + length, phase)
    phase = jnp.where(phase >= length, phase - length, phase)
    angle = (2.0 * math.pi) * phase / length
    return jnp.cos(angle), jnp.sin(angle)


def table_kernel(half_width, scalars, waves_ref, table, turns, coarse_cos, coarse_sin):
    total = waves_ref.shape[1]
    lat = pl.program_id(0)
    row_length = scalars[lat]
    length = jnp.full((1, total), row_length, jnp.int32).astype(jnp.float32)
    wave = waves_ref[...]
    waves = wave.astype(jnp.float32)
    start = scalars[2] * half_width
    weight = jnp.where(wave == 0, 1.0, 2.0)
    weight = jnp.where(wave <= (row_length - 1) // 2, weight, 0.0)
    eight = lax.broadcasted_iota(jnp.int32, (8, total), 0)
    cos_a, sin_a = circle(waves, (eight * BLOCK + start).astype(jnp.float32), length)
    turns[0, 0:8] = cos_a * weight
    turns[0, 8:16] = sin_a * weight
    coarse = lax.broadcasted_iota(jnp.int32, coarse_cos.shape, 0) * 16
    coarse_cos[...], coarse_sin[...] = circle(waves, coarse.astype(jnp.float32), length)
    fine = lax.broadcasted_iota(jnp.int32, (16, total), 0)
    fine_cos, fine_sin = circle(waves, fine.astype(jnp.float32), length)

    @pl.loop(0, table.shape[1] // 16)
    def _(step):
        cos_u, sin_u = coarse_cos[pl.ds(step, 1), :], coarse_sin[pl.ds(step, 1), :]
        at = pl.ds(pl.multiple_of(step * 16, 16), 16)
        table[0, at, 0:total] = (cos_u * fine_cos - sin_u * fine_sin).astype(jnp.bfloat16)
        table[0, at, total:] = (-(sin_u * fine_cos + cos_u * fine_sin)).astype(jnp.bfloat16)


def table_call(scalars, waves, half_width):
    total = waves.shape[1]
    rows = BLOCK + 16
    return pl.pallas_call(
        functools.partial(table_kernel, half_width),
        out_shape=[
            jax.ShapeDtypeStruct((2, rows, 2 * total), jnp.bfloat16),
            jax.ShapeDtypeStruct((2, 16, total), jnp.float32),
        ],
        grid_spec=pltpu.PrefetchScalarGridSpec(
            num_scalar_prefetch=1,
            grid=(2,),
            in_specs=[pl.BlockSpec((1, total), lambda l, s: (0, 0))],
            out_specs=[
                pl.BlockSpec((1, rows, 2 * total), lambda l, s: (l, 0, 0)),
                pl.BlockSpec((1, 16, total), lambda l, s: (l, 0, 0)),
            ],
            scratch_shapes=[pltpu.VMEM((40, total), jnp.float32)] * 2,
        ),
        compiler_params=pltpu.CompilerParams(vmem_limit_bytes=32 << 20),
        cost_estimate=pl.CostEstimate(
            flops=20_000_000, bytes_accessed=6_000_000, transcendentals=400_000
        ),
        name="tables",
    )(scalars, waves)


def fourier_kernel(half_width, fields, count, scalars, *refs):
    arrivals = refs[:count]
    table_ref, turns, out, table, rows, bands, turned, sems = refs[count:]
    total = turns.shape[2]
    lat = pl.program_id(0)
    row_length = scalars[lat]
    lev = scalars[2]
    start = lev * half_width
    pieces = half_width // BLOCK
    copies = [
        pltpu.make_async_copy(table_ref.at[number], table.at[number], sems.at[number])
        for number in (0, 1)
    ]

    @pl.when(lat == 0)
    def _():
        for copy in copies:
            copy.start()
        for number, arrived in enumerate(arrivals):
            rows[number] = arrived[...].astype(jnp.float32).reshape(2048, 128)

    i = lax.broadcasted_iota(jnp.int32, (128, 128), 0)
    j = lax.broadcasted_iota(jnp.int32, (128, 128), 1)
    source = i // 32 * 32 + jnp.where(i % 32 < 16, 2 * (i % 16), 2 * (i % 16) + 1)
    sort = jnp.where(source == j, 1.0, 0.0).astype(jnp.bfloat16)
    for number in range(count):
        for place in range(8):
            part = rows[number, pl.ds(lat * 8 + place, 128, stride=16), :].astype(jnp.bfloat16)
            bands[place * 128 : place * 128 + 128] = lax.dot_general(
                sort, part, NT, preferred_element_type=jnp.float32
            )

        @pl.loop(0, total // 128)
        def _(slot):
            at = pl.ds(pl.multiple_of(slot * 128, 128), 128)
            behind = pl.ds(pl.multiple_of(total + slot * 128, 128), 128)
            base = slot * (2 * fields)
            for third in range(fields // 16):
                real = bands[pl.ds(pl.multiple_of(base + third * 32, 16), 16), :]
                imag = bands[pl.ds(pl.multiple_of(base + third * 32 + 16, 16), 16), :]
                for piece in range(pieces):
                    cos_a = turns[lat, piece : piece + 1, at]
                    sin_a = turns[lat, 8 + piece : 9 + piece, at]
                    row = (number * pieces + piece) * fields + third * 16
                    turned[row : row + 16, at] = (real * cos_a - imag * sin_a).astype(jnp.bfloat16)
                    turned[row : row + 16, behind] = (real * sin_a + imag * cos_a).astype(
                        jnp.bfloat16
                    )

    for number in (0, 1):

        @pl.when(lat == number)
        def _():
            copies[number].wait()

    values = lax.dot_general(
        turned[...], table[lat, 0:BLOCK], NT, preferred_element_type=jnp.float32
    )
    column = lax.broadcasted_iota(jnp.int32, (1, BLOCK), 1) + start
    for number in range(count):
        level = pl.ds(pl.multiple_of((lev if number == 0 else 1 - lev) * fields, 16), fields)
        for piece in range(pieces):
            base = (number * pieces + piece) * fields
            kept = column + piece * BLOCK < row_length
            out[0, level, piece * BLOCK : piece * BLOCK + BLOCK] = jnp.where(
                kept, values[base : base + fields], 0.0
            ).astype(jnp.bfloat16)
        tail = lax.dot_general(
            turned[base : base + fields],
            table[lat, BLOCK : BLOCK + 16],
            NT,
            preferred_element_type=jnp.float32,
        )
        kept = lax.broadcasted_iota(jnp.int32, (1, 16), 1) + (start + pieces * BLOCK) < row_length
        out[0, level, pieces * BLOCK :] = jnp.where(kept, tail, 0.0)[:, 0:8].astype(jnp.bfloat16)


def fourier_call(scalars, arrivals, table, turns, half_width, fields):
    count = len(arrivals)
    pieces = half_width // BLOCK
    return pl.pallas_call(
        functools.partial(fourier_kernel, half_width, fields, count),
        out_shape=jax.ShapeDtypeStruct((2, 2 * fields, half_width), jnp.bfloat16),
        grid_spec=pltpu.PrefetchScalarGridSpec(
            num_scalar_prefetch=1,
            grid=(2,),
            in_specs=[pl.BlockSpec(memory_space=pltpu.VMEM)] * count
            + [pl.BlockSpec(memory_space=pl.ANY), pl.BlockSpec(memory_space=pltpu.VMEM)],
            out_specs=pl.BlockSpec((1, 2 * fields, half_width), lambda l, s: (l, 0, 0)),
            scratch_shapes=[
                pltpu.VMEM(table.shape, jnp.bfloat16),
                pltpu.VMEM((count, 2048, 128), jnp.float32),
                pltpu.VMEM((1024, 128), jnp.float32),
                pltpu.VMEM((count * pieces * fields, table.shape[2]), jnp.bfloat16),
                pltpu.SemaphoreType.DMA((2,)),
            ],
        ),
        compiler_params=pltpu.CompilerParams(vmem_limit_bytes=58 << 20),
        name="fourier",
    )(scalars, *arrivals, table, turns)


def on_device(spectra, legendre, wave_slots, row_length):
    slots = spectra.shape[0]
    fields = spectra.shape[1] // 2
    total = wave_slots.shape[0]
    half_width = (4 * total + 16) // 2
    first = (lax.axis_index("wave") * slots).astype(jnp.int32)[None]
    lev = lax.axis_index("lev").astype(jnp.int32)
    scalars = jnp.concatenate([row_length, lev[None]])
    waves = wave_slots.reshape(total // slots, slots).T.reshape(1, total)
    sent = legendre_call(wave_slots, first, legendre, spectra)
    arrived = lax.all_to_all(sent, "wave", split_axis=0, concat_axis=0, tiled=True)
    table, turns = table_call(scalars, waves, half_width)
    arrived, table, turns = lax.optimization_barrier((arrived, table, turns))
    other = lax.ppermute(arrived, "lev", [(0, 1), (1, 0)])
    return fourier_call(scalars, (arrived, other), table, turns, half_width, fields)


def solution(mesh):
    placed = (P("wave", "lev", None), P("wave", None, None), P(), P("wave"))
    return jax.shard_map(
        on_device, mesh=mesh, in_specs=placed, out_specs=P("wave", None, "lev"), check_vma=False
    )
```

time: 406 us -> 57.5 us (0.14); the launches traced: 399 us -> 57.3 us
  matrix products: 283 us -> 0 us
  local copies, waits for them, and re-layouts: 56.9 us -> 4.05 us
  Pallas kernels: 0 us -> 22.2 us
  other arithmetic: 18.1 us -> 0.08 us
  blocking collectives: 8.68 us -> 0 us
  between operations: 5.78 us -> 0.07 us
    unnamed x8 -> x0, matrix products: 279 us -> none
    pallas_call x0 -> x3, Pallas kernels: none -> 22.2 us  [the longest x1 9.15 us: fourier_call(): pl.pallas_call(functools.partial(fourier_kernel, half_width, fields, coun...]
    unnamed x12 -> x15, local copies, waits for them, and re-layouts: 22.1 us -> 3.86 us
    all_to_all x3 -> x0, local copies, waits for them, and re-layouts: 10.5 us -> none  [the longest x1 6.93 us: on_device(): lax.all_to_all(grid_local, 'lev', split_axis=2, concat_axis=1, tiled=True)]
    all_to_all x1 -> x0, blocking collectives: 8.68 us -> none  [on_device(): lax.all_to_all(grid_local, 'lev', split_axis=2, concat_axis=1, tiled=True)]
    mul x4 -> x0, local copies, waits for them, and re-layouts: 7.29 us -> none  [the longest x2 4 us: half_row(): imag_part = band_imag.astype(jnp.float32) * weights[:, None]]
    another operation x1 -> x0, local copies, waits for them, and re-layouts: 6.53 us -> none  [fourier_rows(): return jnp.stack(results)]
    reshape x5 -> x1, local copies, waits for them, and re-layouts: 6.21 us -> 0.13 us  [on_device(): waves = wave_slots.reshape(total // slots, slots).T.reshape(1, total)]
  transfers between devices with their start and end apart: 1 -> 2, of which waited for: 1 -> 2; matrix products, arithmetic and copies ran while one was open for 1% -> 0% of each run, Pallas kernels for 0% -> 9%
where the time goes in v1:
time: 57.5 us; the launch traced here: 57.3 us
  Pallas kernels  22.2 us (39%)
  starting transfers between devices  18.9 us (33%)
  waiting for transfers between devices  12 us (21%)
  local copies, waits for them, and re-layouts  4.05 us (7%)
    all_to_all x1, starting transfers between devices, on_device(): lax.all_to_all(sent, 'wave', split_axis=0, concat_axis=0, tiled=True)  16.4 us
    all_to_all x1, waiting for transfers between devices, on_device(): lax.all_to_all(sent, 'wave', split_axis=0, concat_axis=0, tiled=True)  10.4 us
    pallas_call x1, Pallas kernels, fourier_call(): pl.pallas_call(functools.partial(fourier_kernel, half_width, fields, coun...  9.15 us
    pallas_call x1, Pallas kernels, legendre_call(): pl.pallas_call(legendre_kernel, out_shape=jax.ShapeDtypeStruct((128, 16,...  7.71 us
    pallas_call x1, Pallas kernels, table_call(): pl.pallas_call(functools.partial(table_kernel, half_width), out_shape=[ja...  5.3 us
    unnamed x15, local copies, waits for them, and re-layouts  3.86 us
    ppermute x1, starting transfers between devices, on_device(): other = lax.ppermute(arrived, 'lev', [(0, 1), (1, 0)])  2.53 us
    ppermute x1, waiting for transfers between devices, on_device(): other = lax.ppermute(arrived, 'lev', [(0, 1), (1, 0)])  1.54 us
  transfers between devices with their start and end apart: 2, of which 2 were waited for; matrix products, arithmetic and copies ran while one was open for 0% of the time, Pallas kernels for 9%

profile of v1, /device:TPU:1, one launch (start us, length us, event | category | flops | bytes accessed | tf_op | source)
XLA Modules:
  0.0 57.3 jit_solution(401832220216604741)
XLA Ops:
  0.0 0.0 copy-start.5
  0.0 0.0 copy-start.6
  0.0 7.7 %legendre.2 = bf16[128,16,128]{2,1,0:T(8,128)(2,1)} custom-call(s32[1280]{0:T(1024)} %waves.1, s32[1]{0:T(128)} %bitcast.1.first, bf16[10,128,1280]{2,1,0:T(8,128)(2,1)} %legendre.3, bf16[10,96,1280]{2,1,0:T(8,128)(2,1)} %spectra.1), custom_call_target="tpu_custom_call" | custom-call | tf_op jit(solution)/shard_map/legendre/pallas_call | solution.py:92
  7.7 16.4 %all-to-all-start = ((bf16[128,16,128]{2,1,0:T(8,128)(2,1)}), bf16[128,16,128]{2,1,0:T(8,128)(2,1)S(1)}, u32[]{:S(2)}, u32[]{:S(2)}) async-start(bf16[128,16,128]{2,1,0:T(8,128)(2,1)} %legendre.2), calls=%async_computation | async-start | bytes 1048576 | tf_op jit(solution)/shard_map/all_to_all | solution.py:285
  24.1 0.0 copy-done.5
  24.1 0.1 reshape.6
  24.3 0.1 copy.5
  24.3 0.0 copy-done.6
  24.4 0.1 pad_add_fusion.scalars
  24.4 0.0 copy-start.2
  24.4 5.3 %tables.1 = (bf16[2,528,2560]{2,1,0:T(8,128)(2,1)S(1)}, f32[2,16,1280]{2,1,0:T(8,128)S(1)}) custom-call(s32[3]{0:T(128)S(1)} %pad_add_fusion.scalars, s32[1,1280]{1,0:T(1,128)S(1)} %bitcast.8), custom_call_target="tpu_custom_call" | custom-call | flops 20000000 | bytes 6000000 | tf_op jit(solution)/shard_map/tables/pallas_call | solution.py:149
  29.7 0.0 copy-start
  29.8 2.4 %copy-done = bf16[2,528,2560]{2,1,0:T(8,128)(2,1)} copy-done((bf16[2,528,2560]{2,1,0:T(8,128)(2,1)}, bf16[2,528,2560]{2,1,0:T(8,128)(2,1)S(1)}, u32[]{:S(2)}) %copy-start) | copy-done | bytes 5406744
  32.1 0.0 copy-start.1
  32.1 0.7 %copy-done.1 = f32[2,16,1280]{2,1,0:T(8,128)} copy-done((f32[2,16,1280]{2,1,0:T(8,128)}, f32[2,16,1280]{2,1,0:T(8,128)S(1)}, u32[]{:S(2)}) %copy-start.1) | copy-done | bytes 163864
  32.8 10.4 %all-to-all-done.refs_0_ = bf16[128,16,128]{2,1,0:T(8,128)(2,1)S(1)} async-done(((bf16[128,16,128]{2,1,0:T(8,128)(2,1)}), bf16[128,16,128]{2,1,0:T(8,128)(2,1)S(1)}, u32[]{:S(2)}, u32[]{:S(2)}) %all-to-all-start) | async-done | bytes 524320 | tf_op jit(solution)/shard_map/all_to_all | solution.py:285
  43.2 0.0 copy-start.3
  43.2 2.5 %collective-permute-start = (bf16[128,16,128]{2,1,0:T(8,128)(2,1)S(1)}, bf16[128,16,128]{2,1,0:T(8,128)(2,1)S(1)}, u32[]{:S(2)}, u32[]{:S(2)}) collective-permute-start(bf16[128,16,128]{2,1,0:T(8,128)(2,1)S(1)} %all-to-all-done.refs_0_), channel_id=1, source_target_pairs={{0,1},{1,0},{2,3},{3,2},{4,5},{5,4},{6,7},{7,6},{8,9},{9,8},{10,11... | collective-permute-start | bytes 1572872 | tf_op jit(solution)/shard_map/ppermute | solution.py:288
  45.8 1.5 %collective-permute-done.refs_1_ = bf16[128,16,128]{2,1,0:T(8,128)(2,1)S(1)} collective-permute-done((bf16[128,16,128]{2,1,0:T(8,128)(2,1)S(1)}, bf16[128,16,128]{2,1,0:T(8,128)(2,1)S(1)}, u32[]{:S(2)}, u32[]{:S(2)}) %collective-permute-start) | collective-permute-done | bytes 524320 | tf_op jit(solution)/shard_map/ppermute | solution.py:288
  47.3 0.0 copy-done.2
  47.3 0.0 copy-done.3
  47.3 0.0 copy-start.4
  47.3 0.8 %copy-done.4 = bf16[128,16,128]{2,1,0:T(8,128)(2,1)} copy-done((bf16[128,16,128]{2,1,0:T(8,128)(2,1)}, bf16[128,16,128]{2,1,0:T(8,128)(2,1)S(1)}, u32[]{:S(2)}) %copy-start.4) | copy-done | bytes 524312
  48.1 9.2 %fourier.1 = bf16[2,96,2568]{2,1,0:T(8,128)(2,1)} custom-call(s32[3]{0:T(128)} %copy-done.2, bf16[128,16,128]{2,1,0:T(8,128)(2,1)} %copy-done.3, bf16[128,16,128]{2,1,0:T(8,128)(2,1)} %copy-done.4, bf16[2,528,2560]{2,1,0:T(8,128)(2,1)} %copy-done, f32[2,16,1280]{2,1,0:T(8,128)} %copy-done.1), custom_call_target="tpu_custom_call" | custom-call | tf_op jit(solution)/shard_map/fourier/pallas_call | solution.py:253
  (1 shorter events, 0.0 us)
Async XLA Ops:
  0.0 24.1 %copy-start.5 = (s32[1280]{0:T(1024)S(1)}, s32[1280]{0:T(1024)}, u32[]{:S(2)}) copy-start(s32[1280]{0:T(1024)} %waves.1) | copy-start | bytes 15364
  0.0 24.3 %copy-start.6 = (s32[2]{0:T(128)S(1)}, s32[2]{0:T(128)}, u32[]{:S(2)}) copy-start(s32[2]{0:T(128)} %param.7) | copy-start | bytes 28
  7.7 35.5 %all-to-all-start = ((bf16[128,16,128]{2,1,0:T(8,128)(2,1)}), bf16[128,16,128]{2,1,0:T(8,128)(2,1)S(1)}, u32[]{:S(2)}, u32[]{:S(2)}) async-start(bf16[128,16,128]{2,1,0:T(8,128)(2,1)} %legendre.2), calls=%async_computation | async-start | bytes 1048576 | tf_op jit(solution)/shard_map/all_to_all | solution.py:285
  24.4 22.9 %copy-start.2 = (s32[3]{0:T(128)}, s32[3]{0:T(128)S(1)}, u32[]{:S(2)}) copy-start(s32[3]{0:T(128)S(1)} %pad_add_fusion.scalars) | copy-start | bytes 40
  29.7 2.4 %copy-start = (bf16[2,528,2560]{2,1,0:T(8,128)(2,1)}, bf16[2,528,2560]{2,1,0:T(8,128)(2,1)S(1)}, u32[]{:S(2)}) copy-start(bf16[2,528,2560]{2,1,0:T(8,128)(2,1)S(1)} %get-tuple-element.13.refs_2_) | copy-start | bytes 16220164
  32.1 0.7 %copy-start.1 = (f32[2,16,1280]{2,1,0:T(8,128)}, f32[2,16,1280]{2,1,0:T(8,128)S(1)}, u32[]{:S(2)}) copy-start(f32[2,16,1280]{2,1,0:T(8,128)S(1)} %get-tuple-element.14.refs_3_) | copy-start | bytes 491524
  43.2 4.1 %copy-start.3 = (bf16[128,16,128]{2,1,0:T(8,128)(2,1)}, bf16[128,16,128]{2,1,0:T(8,128)(2,1)S(1)}, u32[]{:S(2)}) copy-start(bf16[128,16,128]{2,1,0:T(8,128)(2,1)S(1)} %all-to-all-done.refs_0_) | copy-start | bytes 1572868
  43.2 4.1 %collective-permute-start = (bf16[128,16,128]{2,1,0:T(8,128)(2,1)S(1)}, bf16[128,16,128]{2,1,0:T(8,128)(2,1)S(1)}, u32[]{:S(2)}, u32[]{:S(2)}) collective-permute-start(bf16[128,16,128]{2,1,0:T(8,128)(2,1)S(1)} %all-to-all-done.refs_0_), channel_id=1, source_target_pairs={{0,1},{1,0},{2,3},{3,2},{4,5},{5,4},{6,7},{7,6},{8,9},{9,8},{10,11... | collective-permute-start | bytes 1572872 | tf_op jit(solution)/shard_map/ppermute | solution.py:288
  47.3 0.8 %copy-start.4 = (bf16[128,16,128]{2,1,0:T(8,128)(2,1)}, bf16[128,16,128]{2,1,0:T(8,128)(2,1)S(1)}, u32[]{:S(2)}) copy-start(bf16[128,16,128]{2,1,0:T(8,128)(2,1)S(1)} %collective-permute-done.refs_1_) | copy-start | bytes 1572868

commit v2 on v1

v2 whole, which is shorter than its diff:
```python
import functools
import math

import jax
import jax.numpy as jnp
from jax import lax
from jax.experimental import pallas as pl
from jax.experimental.pallas import tpu as pltpu
from jax.sharding import PartitionSpec as P

BLOCK = 512
NT = (((1,), (1,)), ((), ()))
CHUNK = 256


def legendre_kernel(waves_ref, legendre, spectra, sent, waves, tables, spectrum, sums, rows, sems, wave_sem):
    slots, columns, degrees = spectrum.shape
    lats = tables.shape[1]
    steps = degrees // CHUNK + 1
    copies = [
        (
            pltpu.make_async_copy(legendre.at[slot], tables.at[slot], sems.at[slot, 0]),
            pltpu.make_async_copy(spectra.at[slot], spectrum.at[slot], sems.at[slot, 1]),
        )
        for slot in range(slots)
    ]
    fetch = pltpu.make_async_copy(waves_ref, waves, wave_sem)
    fetch.start()
    for both in copies:
        for copy in both:
            copy.start()
    first = lax.axis_index("wave") * slots
    sums[...] = jnp.zeros_like(sums)
    i = lax.broadcasted_iota(jnp.int32, (lats, lats), 0)
    j = lax.broadcasted_iota(jnp.int32, (lats, lats), 1)
    same = jnp.where(i == j, 1.0, 0.0).astype(jnp.bfloat16)
    fetch.wait()
    for pair in range(slots // 2):
        for slot in (2 * pair, 2 * pair + 1):
            for copy in copies[slot]:
                copy.wait()
        wave = waves[first + 2 * pair]
        skipped = wave // CHUNK
        split = steps - 1 - skipped
        for step in range(steps):
            later = step >= split
            slot = 2 * pair + later.astype(jnp.int32)
            start = pl.multiple_of(jnp.where(later, step - 1, skipped + step) * CHUNK, CHUNK)
            number = jnp.where(later, degrees - 1 - wave, wave)
            degree = lax.broadcasted_iota(jnp.int32, (1, CHUNK), 1) + start
            mask = jnp.where(degree >= number // 64 * 64, 1.0, 0.0)
            signed = jnp.where((degree - number) % 2 == 0, mask, -mask).astype(jnp.bfloat16)
            own = spectrum[slot, :, pl.ds(start, CHUNK)]
            both = lax.dot_general(
                jnp.concatenate([own * mask.astype(jnp.bfloat16), own * signed], axis=0),
                tables[slot, :, pl.ds(start, CHUNK)],
                NT,
                preferred_element_type=jnp.float32,
            )
            at = pl.ds(pl.multiple_of(slot * columns, 32), columns)
            sums[0, at, :] += both[0:columns]
            sums[1, at, :] += both[columns:]
        done = [pair * 2 * columns // 128, (pair + 1) * 2 * columns // 128]
        for part in range(done[0], done[1] if pair < slots // 2 - 1 else 8):
            for side in (0, 1):
                rows[pl.ds(side * 1024 + part, lats, stride=8), :] = lax.dot_general(
                    same,
                    sums[side, part * 128 : part * 128 + 128].astype(jnp.bfloat16),
                    NT,
                    preferred_element_type=jnp.float32,
                )
    sent[...] = rows[...].astype(jnp.bfloat16).reshape(sent.shape)


def legendre_call(waves, legendre, spectra):
    slots, lats, degrees = legendre.shape
    columns = spectra.shape[1]
    return pl.pallas_call(
        legendre_kernel,
        out_shape=jax.ShapeDtypeStruct((128, 16, 128), jnp.bfloat16),
        in_specs=[pl.BlockSpec(memory_space=pl.ANY)] * 3,
        out_specs=pl.BlockSpec(memory_space=pltpu.VMEM),
        scratch_shapes=[
            pltpu.SMEM(waves.shape, jnp.int32),
            pltpu.VMEM((slots, lats, degrees), jnp.bfloat16),
            pltpu.VMEM((slots, columns, degrees), jnp.bfloat16),
            pltpu.VMEM((2, 1024, lats), jnp.float32),
            pltpu.VMEM((2048, 128), jnp.float32),
            pltpu.SemaphoreType.DMA((slots, 2)),
            pltpu.SemaphoreType.DMA,
        ],
        compiler_params=pltpu.CompilerParams(vmem_limit_bytes=60 << 20),
        name="legendre",
    )(waves, legendre, spectra)


def circle(waves, starts, length):
    whole = waves * starts
    turns = jnp.floor(whole * (1.0 / length))
    phase = whole - turns * length
    phase = jnp.where(phase < 0.0, phase + length, phase)
    phase = jnp.where(phase >= length, phase - length, phase)
    angle = (2.0 * math.pi) * phase / length
    return jnp.cos(angle), jnp.sin(angle)


def table_kernel(half_width, scalars, waves_ref, table, turns, coarse_cos, coarse_sin):
    total = waves_ref.shape[1]
    lat = pl.program_id(0)
    row_length = scalars[lat]
    length = jnp.full((1, total), row_length, jnp.int32).astype(jnp.float32)
    wave = waves_ref[...]
    waves = wave.astype(jnp.float32)
    start = scalars[2] * half_width
    weight = jnp.where(wave == 0, 1.0, 2.0)
    weight = jnp.where(wave <= (row_length - 1) // 2, weight, 0.0)
    eight = lax.broadcasted_iota(jnp.int32, (8, total), 0)
    cos_a, sin_a = circle(waves, (eight * BLOCK + start).astype(jnp.float32), length)
    turns[0, 0:8] = cos_a * weight
    turns[0, 8:16] = sin_a * weight
    coarse = lax.broadcasted_iota(jnp.int32, coarse_cos.shape, 0) * 16
    coarse_cos[...], coarse_sin[...] = circle(waves, coarse.astype(jnp.float32), length)
    fine = lax.broadcasted_iota(jnp.int32, (16, total), 0)
    fine_cos, fine_sin = circle(waves, fine.astype(jnp.float32), length)

    @pl.loop(0, table.shape[1] // 16)
    def _(step):
        cos_u, sin_u = coarse_cos[pl.ds(step, 1), :], coarse_sin[pl.ds(step, 1), :]
        at = pl.ds(pl.multiple_of(step * 16, 16), 16)
        table[0, at, 0:total] = (cos_u * fine_cos - sin_u * fine_sin).astype(jnp.bfloat16)
        table[0, at, total:] = (-(sin_u * fine_cos + cos_u * fine_sin)).astype(jnp.bfloat16)


def table_call(scalars, waves, half_width):
    total = waves.shape[1]
    rows = BLOCK + 16
    return pl.pallas_call(
        functools.partial(table_kernel, half_width),
        out_shape=[
            jax.ShapeDtypeStruct((2, rows, 2 * total), jnp.bfloat16),
            jax.ShapeDtypeStruct((2, 16, total), jnp.float32),
        ],
        grid_spec=pltpu.PrefetchScalarGridSpec(
            num_scalar_prefetch=1,
            grid=(2,),
            in_specs=[pl.BlockSpec((1, total), lambda l, s: (0, 0))],
            out_specs=[
                pl.BlockSpec((1, rows, 2 * total), lambda l, s: (l, 0, 0)),
                pl.BlockSpec((1, 16, total), lambda l, s: (l, 0, 0)),
            ],
            scratch_shapes=[pltpu.VMEM((40, total), jnp.float32)] * 2,
        ),
        compiler_params=pltpu.CompilerParams(vmem_limit_bytes=32 << 20),
        cost_estimate=pl.CostEstimate(
            flops=20_000_000, bytes_accessed=6_000_000, transcendentals=400_000
        ),
        name="tables",
    )(scalars, waves)


def fourier_kernel(
    fields,
    lengths_ref,
    own,
    other,
    table_ref,
    turns_ref,
    out_ref,
    lengths,
    arrived,
    table,
    turns,
    rows,
    parts,
    bands,
    first,
    second,
    out,
    sems,
):
    half_width = out.shape[2]
    total = turns.shape[2]
    pieces = half_width // BLOCK
    thirds = fields // 16
    half = BLOCK // 2
    lev = lax.axis_index("lev")
    start = lev * half_width
    fetch = [
        pltpu.make_async_copy(own, arrived.at[0], sems.at[0]),
        pltpu.make_async_copy(other, arrived.at[1], sems.at[1]),
        pltpu.make_async_copy(turns_ref, turns, sems.at[2]),
        pltpu.make_async_copy(lengths_ref, lengths, sems.at[3]),
    ]
    tables = [
        pltpu.make_async_copy(table_ref.at[lat], table.at[lat], sems.at[4 + lat]) for lat in (0, 1)
    ]
    results = [
        pltpu.make_async_copy(out.at[lat], out_ref.at[lat], sems.at[6 + lat]) for lat in (0, 1)
    ]
    for copy in fetch:
        copy.start()
    tables[0].start()
    i = lax.broadcasted_iota(jnp.int32, (128, 128), 0)
    j = lax.broadcasted_iota(jnp.int32, (128, 128), 1)
    source = i // 32 * 32 + jnp.where(i % 32 < 16, 2 * (i % 16), 2 * (i % 16) + 1)
    sort = jnp.where(source == j, 1.0, 0.0).astype(jnp.bfloat16)
    for number in (0, 1):
        fetch[number].wait()
        if number == 1:
            tables[1].start()
        rows[number] = arrived[number].astype(jnp.float32).reshape(2048, 128)
        for lat in (0, 1):
            for place in range(8):
                parts[lat, number, place * 128 : place * 128 + 128] = rows[
                    number, pl.ds(lat * 8 + place, 128, stride=16), :
                ].astype(jnp.bfloat16)
            bands[lat, number] = lax.dot_general(
                sort, parts[lat, number], NT, preferred_element_type=jnp.float32
            )

    def turn(lat, slot, turned):
        at = pl.ds(pl.multiple_of(slot * 128, 128), 128)
        behind = pl.ds(pl.multiple_of(total + slot * 128, 128), 128)
        for third in range(thirds):
            group = slot * thirds + third
            lanes = pl.ds(pl.multiple_of(group // 4 * 128, 128), 128)
            base = pl.multiple_of(group % 4 * 32, 32)
            for number in (0, 1):
                real = bands[lat, number, pl.ds(base, 16), lanes]
                imag = bands[lat, number, pl.ds(base + 16, 16), lanes]
                for piece in range(pieces):
                    cos_a = turns[lat, piece : piece + 1, at]
                    sin_a = turns[lat, 8 + piece : 9 + piece, at]
                    row = (piece * 2 + number) * fields + third * 16
                    turned[row : row + 16, at] = (real * cos_a - imag * sin_a).astype(jnp.bfloat16)
                    turned[row : row + 16, behind] = (real * sin_a + imag * cos_a).astype(
                        jnp.bfloat16
                    )

    def levels(number):
        return pl.ds(pl.multiple_of((lev if number == 0 else 1 - lev) * fields, 16), fields)

    def multiply(lat, side, turned):
        behind = pl.multiple_of(side * half, half)
        values = lax.dot_general(
            turned[...], table[lat, pl.ds(behind, half), :], NT, preferred_element_type=jnp.float32
        )
        column = lax.broadcasted_iota(jnp.int32, (1, half), 1) + (start + behind)
        for piece in range(pieces):
            kept = column + piece * BLOCK < lengths[lat]
            for number in (0, 1):
                row = (piece * 2 + number) * fields
                out[lat, levels(number), pl.ds(piece * BLOCK + behind, half)] = jnp.where(
                    kept, values[row : row + fields], 0.0
                ).astype(jnp.bfloat16)

    def finish(lat, turned):
        tail = lax.dot_general(
            turned[(pieces - 1) * 2 * fields :],
            table[lat, BLOCK : BLOCK + 16],
            NT,
            preferred_element_type=jnp.float32,
        )
        column = lax.broadcasted_iota(jnp.int32, (1, 16), 1) + (start + pieces * BLOCK)
        tail = jnp.where(column < lengths[lat], tail, 0.0)[:, 0 : half_width - pieces * BLOCK]
        for number in (0, 1):
            out[lat, levels(number), pieces * BLOCK :] = tail[
                number * fields : number * fields + fields
            ].astype(jnp.bfloat16)
        results[lat].start()

    fetch[2].wait()
    fetch[3].wait()

    @pl.loop(0, total // 128)
    def _(slot):
        turn(0, slot, first)

    tables[0].wait()
    count = total // 128 // 2

    @pl.loop(0, 2)
    def _(side):
        for step in range(count):
            turn(1, side * count + step, second)
        multiply(0, side, first)

    finish(0, first)
    tables[1].wait()

    @pl.loop(0, 2)
    def _(side):
        multiply(1, side, second)

    finish(1, second)
    results[0].wait()
    results[1].wait()


def fourier_call(lengths, own, other, table, turns, half_width, fields):
    pieces = half_width // BLOCK
    turned = pltpu.VMEM((2 * pieces * fields, table.shape[2]), jnp.bfloat16)
    shape = (2, 2 * fields, half_width)
    return pl.pallas_call(
        functools.partial(fourier_kernel, fields),
        out_shape=jax.ShapeDtypeStruct(shape, jnp.bfloat16),
        in_specs=[pl.BlockSpec(memory_space=pl.ANY)] * 5,
        out_specs=pl.BlockSpec(memory_space=pl.ANY),
        scratch_shapes=[
            pltpu.SMEM((2,), jnp.int32),
            pltpu.VMEM((2,) + own.shape, jnp.bfloat16),
            pltpu.VMEM(table.shape, jnp.bfloat16),
            pltpu.VMEM(turns.shape, jnp.float32),
            pltpu.VMEM((2, 2048, 128), jnp.float32),
            pltpu.VMEM((2, 2, 1024, 128), jnp.bfloat16),
            pltpu.VMEM((2, 2, 128, 1024), jnp.float32),
            turned,
            turned,
            pltpu.VMEM(shape, jnp.bfloat16),
            pltpu.SemaphoreType.DMA((8,)),
        ],
        compiler_params=pltpu.CompilerParams(vmem_limit_bytes=58 << 20),
        name="fourier",
    )(lengths, own, other, table, turns)


def on_device(spectra, legendre, wave_slots, row_length):
    slots = spectra.shape[0]
    fields = spectra.shape[1] // 2
    total = wave_slots.shape[0]
    half_width = (4 * total + 16) // 2
    lev = lax.axis_index("lev").astype(jnp.int32)
    scalars = jnp.concatenate([row_length, lev[None]])
    waves = wave_slots.reshape(total // slots, slots).T.reshape(1, total)
    sent = legendre_call(wave_slots, legendre, spectra)
    arrived = lax.all_to_all(sent, "wave", split_axis=0, concat_axis=0, tiled=True)
    table, turns = table_call(scalars, waves, half_width)
    arrived, table, turns = lax.optimization_barrier((arrived, table, turns))
    other = lax.ppermute(arrived, "lev", [(0, 1), (1, 0)])
    return fourier_call(row_length, arrived, other, table, turns, half_width, fields)


def solution(mesh):
    placed = (P("wave", "lev", None), P("wave", None, None), P(), P("wave"))
    return jax.shard_map(
        on_device, mesh=mesh, in_specs=placed, out_specs=P("wave", None, "lev"), check_vma=False
    )
```

time: 57.5 us -> 53.9 us (0.937)
  Pallas kernels: 22.2 us -> 18.6 us
    pallas_call x1, Pallas kernels: 7.71 us -> 5.11 us  [legendre_call(): pl.pallas_call(legendre_kernel, out_shape=jax.ShapeDtypeStruct((128, 16,...]
    pallas_call x1, Pallas kernels: 9.15 us -> 8.24 us  [fourier_call(): pl.pallas_call(functools.partial(fourier_kernel, fields), out_shape=jax.S...]
    unnamed x15 -> x13, local copies, waits for them, and re-layouts: 3.86 us -> 3.84 us
  transfers between devices with their start and end apart: 2 -> 2, of which waited for: 2 -> 2; matrix products, arithmetic and copies ran while one was open for 0% -> 1% of each run, Pallas kernels for 9% -> 10%
where the time goes in v2:
time: 53.9 us; the launch traced here: 53.7 us
  starting transfers between devices  18.9 us (35%)
  Pallas kernels  18.6 us (35%)
  waiting for transfers between devices  12 us (22%)
  local copies, waits for them, and re-layouts  4.04 us (7%)
    all_to_all x1, starting transfers between devices, on_device(): lax.all_to_all(sent, 'wave', split_axis=0, concat_axis=0, tiled=True)  16.3 us
    all_to_all x1, waiting for transfers between devices, on_device(): lax.all_to_all(sent, 'wave', split_axis=0, concat_axis=0, tiled=True)  10.5 us
    pallas_call x1, Pallas kernels, fourier_call(): pl.pallas_call(functools.partial(fourier_kernel, fields), out_shape=jax.S...  8.24 us
    pallas_call x1, Pallas kernels, table_call(): pl.pallas_call(functools.partial(table_kernel, half_width), out_shape=[ja...  5.3 us
    pallas_call x1, Pallas kernels, legendre_call(): pl.pallas_call(legendre_kernel, out_shape=jax.ShapeDtypeStruct((128, 16,...  5.11 us
    unnamed x13, local copies, waits for them, and re-layouts  3.84 us
    ppermute x1, starting transfers between devices, on_device(): other = lax.ppermute(arrived, 'lev', [(0, 1), (1, 0)])  2.53 us
    ppermute x1, waiting for transfers between devices, on_device(): other = lax.ppermute(arrived, 'lev', [(0, 1), (1, 0)])  1.54 us
  transfers between devices with their start and end apart: 2, of which 2 were waited for; matrix products, arithmetic and copies ran while one was open for 1% of the time, Pallas kernels for 10%

profile of v2, /device:TPU:1, one launch (start us, length us, event | category | flops | bytes accessed | tf_op | source)
XLA Modules:
  0.0 53.7 jit_solution(7319523317139107208)
XLA Ops:
  0.0 0.0 copy-start.4
  0.0 0.0 copy-start.5
  0.0 5.1 %legendre.2 = bf16[128,16,128]{2,1,0:T(8,128)(2,1)} custom-call(s32[1280]{0:T(1024)} %waves_ref.1, bf16[10,128,1280]{2,1,0:T(8,128)(2,1)} %legendre.3, bf16[10,96,1280]{2,1,0:T(8,128)(2,1)} %spectra.1), custom_call_target="tpu_custom_call" | custom-call | tf_op jit(solution)/shard_map/legendre/pallas_call | solution.py:78
  5.1 16.3 %all-to-all-start = ((bf16[128,16,128]{2,1,0:T(8,128)(2,1)}), bf16[128,16,128]{2,1,0:T(8,128)(2,1)S(1)}, u32[]{:S(2)}, u32[]{:S(2)}) async-start(bf16[128,16,128]{2,1,0:T(8,128)(2,1)} %legendre.2), calls=%async_computation | async-start | bytes 1048576 | tf_op jit(solution)/shard_map/all_to_all | solution.py:336
  21.5 0.0 copy-done.4
  21.5 0.1 reshape.6
  21.6 0.1 copy.5
  21.7 0.0 copy-done.5
  21.7 0.1 pad_add_fusion.scalars
  21.8 5.3 %tables.1 = (bf16[2,528,2560]{2,1,0:T(8,128)(2,1)S(1)}, f32[2,16,1280]{2,1,0:T(8,128)S(1)}) custom-call(s32[3]{0:T(128)S(1)} %pad_add_fusion.scalars, s32[1,1280]{1,0:T(1,128)S(1)} %bitcast.7), custom_call_target="tpu_custom_call" | custom-call | flops 20000000 | bytes 6000000 | tf_op jit(solution)/shard_map/tables/pallas_call | solution.py:137
  27.1 0.0 copy-start
  27.1 2.3 %copy-done = bf16[2,528,2560]{2,1,0:T(8,128)(2,1)} copy-done((bf16[2,528,2560]{2,1,0:T(8,128)(2,1)}, bf16[2,528,2560]{2,1,0:T(8,128)(2,1)S(1)}, u32[]{:S(2)}) %copy-start) | copy-done | bytes 5406744
  29.5 0.0 copy-start.1
  29.5 0.7 %copy-done.1 = f32[2,16,1280]{2,1,0:T(8,128)} copy-done((f32[2,16,1280]{2,1,0:T(8,128)}, f32[2,16,1280]{2,1,0:T(8,128)S(1)}, u32[]{:S(2)}) %copy-start.1) | copy-done | bytes 163864
  30.1 10.5 %all-to-all-done.own = bf16[128,16,128]{2,1,0:T(8,128)(2,1)S(1)} async-done(((bf16[128,16,128]{2,1,0:T(8,128)(2,1)}), bf16[128,16,128]{2,1,0:T(8,128)(2,1)S(1)}, u32[]{:S(2)}, u32[]{:S(2)}) %all-to-all-start) | async-done | bytes 524320 | tf_op jit(solution)/shard_map/all_to_all | solution.py:336
  40.6 0.0 copy-start.2
  40.6 2.5 %collective-permute-start = (bf16[128,16,128]{2,1,0:T(8,128)(2,1)S(1)}, bf16[128,16,128]{2,1,0:T(8,128)(2,1)S(1)}, u32[]{:S(2)}, u32[]{:S(2)}) collective-permute-start(bf16[128,16,128]{2,1,0:T(8,128)(2,1)S(1)} %all-to-all-done.own), channel_id=1, source_target_pairs={{0,1},{1,0},{2,3},{3,2},{4,5},{5,4},{6,7},{7,6},{8,9},{9,8},{10,11... | collective-permute-start | bytes 1572872 | tf_op jit(solution)/shard_map/ppermute | solution.py:339
  43.1 1.5 %collective-permute-done.other = bf16[128,16,128]{2,1,0:T(8,128)(2,1)S(1)} collective-permute-done((bf16[128,16,128]{2,1,0:T(8,128)(2,1)S(1)}, bf16[128,16,128]{2,1,0:T(8,128)(2,1)S(1)}, u32[]{:S(2)}, u32[]{:S(2)}) %collective-permute-start) | collective-permute-done | bytes 524320 | tf_op jit(solution)/shard_map/ppermute | solution.py:339
  44.7 0.0 copy-done.2
  44.7 0.0 copy-start.3
  44.7 0.8 %copy-done.3 = bf16[128,16,128]{2,1,0:T(8,128)(2,1)} copy-done((bf16[128,16,128]{2,1,0:T(8,128)(2,1)}, bf16[128,16,128]{2,1,0:T(8,128)(2,1)S(1)}, u32[]{:S(2)}) %copy-start.3) | copy-done | bytes 524312
  45.5 8.2 %fourier.1 = bf16[2,96,2568]{2,1,0:T(8,128)(2,1)} custom-call(s32[2]{0:T(128)} %lengths_ref.1, bf16[128,16,128]{2,1,0:T(8,128)(2,1)} %copy-done.2, bf16[128,16,128]{2,1,0:T(8,128)(2,1)} %copy-done.3, bf16[2,528,2560]{2,1,0:T(8,128)(2,1)} %copy-done, f32[2,16,1280]{2,1,0:T(8,128)} %copy-done.1), custom_call_target="tpu_custom_call" | custom-call | tf_op jit(solution)/shard_map/fourier/pallas_call | solution.py:304
  (1 shorter events, 0.0 us)
Async XLA Ops:
  0.0 21.5 %copy-start.4 = (s32[1280]{0:T(1024)S(1)}, s32[1280]{0:T(1024)}, u32[]{:S(2)}) copy-start(s32[1280]{0:T(1024)} %waves_ref.1) | copy-start | bytes 15364
  0.0 21.7 %copy-start.5 = (s32[2]{0:T(128)S(1)}, s32[2]{0:T(128)}, u32[]{:S(2)}) copy-start(s32[2]{0:T(128)} %lengths_ref.1) | copy-start | bytes 28
  5.1 35.5 %all-to-all-start = ((bf16[128,16,128]{2,1,0:T(8,128)(2,1)}), bf16[128,16,128]{2,1,0:T(8,128)(2,1)S(1)}, u32[]{:S(2)}, u32[]{:S(2)}) async-start(bf16[128,16,128]{2,1,0:T(8,128)(2,1)} %legendre.2), calls=%async_computation | async-start | bytes 1048576 | tf_op jit(solution)/shard_map/all_to_all | solution.py:336
  27.1 2.4 %copy-start = (bf16[2,528,2560]{2,1,0:T(8,128)(2,1)}, bf16[2,528,2560]{2,1,0:T(8,128)(2,1)S(1)}, u32[]{:S(2)}) copy-start(bf16[2,528,2560]{2,1,0:T(8,128)(2,1)S(1)} %get-tuple-element.13.table_ref) | copy-start | bytes 16220164
  29.5 0.7 %copy-start.1 = (f32[2,16,1280]{2,1,0:T(8,128)}, f32[2,16,1280]{2,1,0:T(8,128)S(1)}, u32[]{:S(2)}) copy-start(f32[2,16,1280]{2,1,0:T(8,128)S(1)} %get-tuple-element.14.turns_ref) | copy-start | bytes 491524
  40.6 4.1 %copy-start.2 = (bf16[128,16,128]{2,1,0:T(8,128)(2,1)}, bf16[128,16,128]{2,1,0:T(8,128)(2,1)S(1)}, u32[]{:S(2)}) copy-start(bf16[128,16,128]{2,1,0:T(8,128)(2,1)S(1)} %all-to-all-done.own) | copy-start | bytes 1572868
  40.6 4.1 %collective-permute-start = (bf16[128,16,128]{2,1,0:T(8,128)(2,1)S(1)}, bf16[128,16,128]{2,1,0:T(8,128)(2,1)S(1)}, u32[]{:S(2)}, u32[]{:S(2)}) collective-permute-start(bf16[128,16,128]{2,1,0:T(8,128)(2,1)S(1)} %all-to-all-done.own), channel_id=1, source_target_pairs={{0,1},{1,0},{2,3},{3,2},{4,5},{5,4},{6,7},{7,6},{8,9},{9,8},{10,11... | collective-permute-start | bytes 1572872 | tf_op jit(solution)/shard_map/ppermute | solution.py:339
  44.7 0.8 %copy-start.3 = (bf16[128,16,128]{2,1,0:T(8,128)(2,1)}, bf16[128,16,128]{2,1,0:T(8,128)(2,1)S(1)}, u32[]{:S(2)}) copy-start(bf16[128,16,128]{2,1,0:T(8,128)(2,1)S(1)} %collective-permute-done.other) | copy-start | bytes 1572868

commit v3 on v2

--- a/solution.py
+++ b/solution.py
@@ -9,6 +9,8 @@
 from jax.sharding import PartitionSpec as P
 
 BLOCK = 512
+PIECES = 5
+VMEM = 48 << 20
 NT = (((1,), (1,)), ((), ()))
 CHUNK = 256
 
@@ -158,170 +160,183 @@
     )(scalars, waves)
 
 
+def unpack(arrived, rows, parts, keep):
+    rows[...] = arrived[...].astype(jnp.float32).reshape(2048, 128)
+    i = lax.broadcasted_iota(jnp.int32, (128, 128), 0)
+    j = lax.broadcasted_iota(jnp.int32, (128, 128), 1)
+    source = i // 32 * 32 + jnp.where(i % 32 < 16, 2 * (i % 16), 2 * (i % 16) + 1)
+    sort = jnp.where(source == j, 1.0, 0.0).astype(jnp.bfloat16)
+    for lat in (0, 1):
+        for place in range(8):
+            parts[lat, place * 128 : place * 128 + 128] = rows[
+                pl.ds(lat * 8 + place, 128, stride=16), :
+            ].astype(jnp.bfloat16)
+        keep[lat][...] = lax.dot_general(sort, parts[lat], NT, preferred_element_type=jnp.float32)
+
+
+def turn(bands, turns, lat, slot, turned):
+    total = turns.shape[2]
+    fields = turned.shape[0] // PIECES
+    at = pl.ds(pl.multiple_of(slot * 128, 128), 128)
+    behind = pl.ds(pl.multiple_of(total + slot * 128, 128), 128)
+    for third in range(fields // 16):
+        group = slot * (fields // 16) + third
+        lanes = pl.ds(pl.multiple_of(group // 4 * 128, 128), 128)
+        base = pl.multiple_of(group % 4 * 32, 32)
+        real = bands[pl.ds(base, 16), lanes]
+        imag = bands[pl.ds(base + 16, 16), lanes]
+        for piece in range(PIECES):
+            cos_a = turns[lat, piece : piece + 1, at]
+            sin_a = turns[lat, 8 + piece : 9 + piece, at]
+            row = piece * fields + third * 16
+            turned[row : row + 16, at] = (real * cos_a - imag * sin_a).astype(jnp.bfloat16)
+            turned[row : row + 16, behind] = (real * sin_a + imag * cos_a).astype(jnp.bfloat16)
+
+
+def own_kernel(
+    lengths, own, table_ref, turns_ref, turned, table, turns, limits, rows, parts, bands, sems
+):
+    fetch = [
+        pltpu.make_async_copy(turns_ref, turns, sems.at[0]),
+        pltpu.make_async_copy(table_ref.at[0], table, sems.at[1]),
+    ]
+    for copy in fetch:
+        copy.start()
+    for lat in (0, 1):
+        limits[8 * lat : 8 * lat + 8] = jnp.full((8, BLOCK), lengths[lat], jnp.int32)
+    unpack(own, rows, parts, (bands.at[0], bands.at[1]))
+    fetch[0].wait()
+
+    @pl.loop(0, turns.shape[2] // 128)
+    def _(slot):
+        for lat in (0, 1):
+            turn(bands.at[lat], turns, lat, slot, turned.at[lat])
+
+    fetch[1].wait()
+
+
+def own_call(lengths, own, table, turns, fields):
+    return pl.pallas_call(
+        own_kernel,
+        out_shape=[
+            jax.ShapeDtypeStruct((2, PIECES * fields, table.shape[2]), jnp.bfloat16),
+            jax.ShapeDtypeStruct(table.shape[1:], jnp.bfloat16),
+            jax.ShapeDtypeStruct(turns.shape, jnp.float32),
+            jax.ShapeDtypeStruct((16, BLOCK), jnp.int32),
+        ],
+        in_specs=[
+            pl.BlockSpec(memory_space=pltpu.SMEM),
+            pl.BlockSpec(memory_space=pltpu.VMEM),
+            pl.BlockSpec(memory_space=pl.ANY),
+            pl.BlockSpec(memory_space=pl.ANY),
+        ],
+        out_specs=[pl.BlockSpec(memory_space=pltpu.VMEM)] * 4,
+        scratch_shapes=[
+            pltpu.VMEM((2048, 128), jnp.float32),
+            pltpu.VMEM((2, 1024, 128), jnp.bfloat16),
+            pltpu.VMEM((2, 128, 1024), jnp.float32),
+            pltpu.SemaphoreType.DMA((2,)),
+        ],
+        compiler_params=pltpu.CompilerParams(vmem_limit_bytes=VMEM),
+        cost_estimate=pl.CostEstimate(
+            flops=40_000_000, bytes_accessed=6_000_000, transcendentals=0
+        ),
+        name="own",
+    )(lengths, own, table, turns)
+
+
 def fourier_kernel(
     fields,
-    lengths_ref,
-    own,
+    own_turned,
     other,
+    table_north,
+    turns,
+    limits,
     table_ref,
-    turns_ref,
     out_ref,
-    lengths,
-    arrived,
-    table,
-    turns,
+    table_south,
     rows,
     parts,
     bands,
-    first,
-    second,
+    turned,
     out,
     sems,
 ):
     half_width = out.shape[2]
-    total = turns.shape[2]
-    pieces = half_width // BLOCK
-    thirds = fields // 16
-    half = BLOCK // 2
+    slots = turns.shape[2] // 128
     lev = lax.axis_index("lev")
     start = lev * half_width
-    fetch = [
-        pltpu.make_async_copy(own, arrived.at[0], sems.at[0]),
-        pltpu.make_async_copy(other, arrived.at[1], sems.at[1]),
-        pltpu.make_async_copy(turns_ref, turns, sems.at[2]),
-        pltpu.make_async_copy(lengths_ref, lengths, sems.at[3]),
-    ]
-    tables = [
-        pltpu.make_async_copy(table_ref.at[lat], table.at[lat], sems.at[4 + lat]) for lat in (0, 1)
-    ]
-    results = [
-        pltpu.make_async_copy(out.at[lat], out_ref.at[lat], sems.at[6 + lat]) for lat in (0, 1)
-    ]
-    for copy in fetch:
-        copy.start()
-    tables[0].start()
-    i = lax.broadcasted_iota(jnp.int32, (128, 128), 0)
-    j = lax.broadcasted_iota(jnp.int32, (128, 128), 1)
-    source = i // 32 * 32 + jnp.where(i % 32 < 16, 2 * (i % 16), 2 * (i % 16) + 1)
-    sort = jnp.where(source == j, 1.0, 0.0).astype(jnp.bfloat16)
-    for number in (0, 1):
-        fetch[number].wait()
-        if number == 1:
-            tables[1].start()
-        rows[number] = arrived[number].astype(jnp.float32).reshape(2048, 128)
-        for lat in (0, 1):
-            for place in range(8):
-                parts[lat, number, place * 128 : place * 128 + 128] = rows[
-                    number, pl.ds(lat * 8 + place, 128, stride=16), :
-                ].astype(jnp.bfloat16)
-            bands[lat, number] = lax.dot_general(
-                sort, parts[lat, number], NT, preferred_element_type=jnp.float32
-            )
-
-    def turn(lat, slot, turned):
-        at = pl.ds(pl.multiple_of(slot * 128, 128), 128)
-        behind = pl.ds(pl.multiple_of(total + slot * 128, 128), 128)
-        for third in range(thirds):
-            group = slot * thirds + third
-            lanes = pl.ds(pl.multiple_of(group // 4 * 128, 128), 128)
-            base = pl.multiple_of(group % 4 * 32, 32)
-            for number in (0, 1):
-                real = bands[lat, number, pl.ds(base, 16), lanes]
-                imag = bands[lat, number, pl.ds(base + 16, 16), lanes]
-                for piece in range(pieces):
-                    cos_a = turns[lat, piece : piece + 1, at]
-                    sin_a = turns[lat, 8 + piece : 9 + piece, at]
-                    row = (piece * 2 + number) * fields + third * 16
-                    turned[row : row + 16, at] = (real * cos_a - imag * sin_a).astype(jnp.bfloat16)
-                    turned[row : row + 16, behind] = (real * sin_a + imag * cos_a).astype(
-                        jnp.bfloat16
-                    )
-
-    def levels(number):
-        return pl.ds(pl.multiple_of((lev if number == 0 else 1 - lev) * fields, 16), fields)
-
-    def multiply(lat, side, turned):
-        behind = pl.multiple_of(side * half, half)
+    fetch = pltpu.make_async_copy(table_ref.at[1], table_south, sems.at[0])
+    fetch.start()
+
+    def multiply(lat, number, lines, beside=None):
+        table = table_south if lat else table_north
         values = lax.dot_general(
-            turned[...], table[lat, pl.ds(behind, half), :], NT, preferred_element_type=jnp.float32
+            lines[...], table[0:BLOCK], NT, preferred_element_type=jnp.float32
         )
-        column = lax.broadcasted_iota(jnp.int32, (1, half), 1) + (start + behind)
-        for piece in range(pieces):
-            kept = column + piece * BLOCK < lengths[lat]
-            for number in (0, 1):
-                row = (piece * 2 + number) * fields
-                out[lat, levels(number), pl.ds(piece * BLOCK + behind, half)] = jnp.where(
-                    kept, values[row : row + fields], 0.0
-                ).astype(jnp.bfloat16)
-
-    def finish(lat, turned):
         tail = lax.dot_general(
-            turned[(pieces - 1) * 2 * fields :],
-            table[lat, BLOCK : BLOCK + 16],
+            lines[(PIECES - 1) * fields :, :],
+            table[BLOCK : BLOCK + 16],
             NT,
             preferred_element_type=jnp.float32,
         )
-        column = lax.broadcasted_iota(jnp.int32, (1, 16), 1) + (start + pieces * BLOCK)
-        tail = jnp.where(column < lengths[lat], tail, 0.0)[:, 0 : half_width - pieces * BLOCK]
-        for number in (0, 1):
-            out[lat, levels(number), pieces * BLOCK :] = tail[
-                number * fields : number * fields + fields
-            ].astype(jnp.bfloat16)
-        results[lat].start()
-
-    fetch[2].wait()
-    fetch[3].wait()
-
-    @pl.loop(0, total // 128)
-    def _(slot):
-        turn(0, slot, first)
-
-    tables[0].wait()
-    count = total // 128 // 2
-
-    @pl.loop(0, 2)
-    def _(side):
-        for step in range(count):
-            turn(1, side * count + step, second)
-        multiply(0, side, first)
-
-    finish(0, first)
-    tables[1].wait()
-
-    @pl.loop(0, 2)
-    def _(side):
-        multiply(1, side, second)
-
-    finish(1, second)
-    results[0].wait()
-    results[1].wait()
-
-
-def fourier_call(lengths, own, other, table, turns, half_width, fields):
-    pieces = half_width // BLOCK
-    turned = pltpu.VMEM((2 * pieces * fields, table.shape[2]), jnp.bfloat16)
+        if beside is not None:
+            beside()
+        level = pl.ds(pl.multiple_of((number ^ lev) * fields, 16), fields)
+        column = lax.broadcasted_iota(jnp.int32, (1, BLOCK), 1) + start
+        limit = limits[8 * lat : 8 * lat + 1]
+        for piece in range(PIECES):
+            out[lat, level, piece * BLOCK : piece * BLOCK + BLOCK] = jnp.where(
+                column + piece * BLOCK < limit, values[piece * fields : piece * fields + fields], 0.0
+            ).astype(jnp.bfloat16)
+        kept = column[:, 0:16] + PIECES * BLOCK < limit[:, 0:16]
+        out[lat, level, PIECES * BLOCK :] = jnp.where(kept, tail, 0.0)[
+            :, 0 : half_width - PIECES * BLOCK
+        ].astype(jnp.bfloat16)
+        copy = pltpu.make_async_copy(
+            out.at[lat, level], out_ref.at[lat, level], sems.at[1 + 2 * lat + number]
+        )
+        copy.start()
+        return copy
+
+    def turn_other(lat):
+        for slot in range(slots):
+            turn(bands.at[lat], turns, lat, slot, turned.at[lat])
+
+    def open_other():
+        unpack(other, rows, parts, (bands.at[0], bands.at[1]))
+        turn_other(0)
+
+    copies = [
+        multiply(0, 0, own_turned.at[0], open_other),
+        multiply(0, 1, turned.at[0], lambda: turn_other(1)),
+    ]
+    fetch.wait()
+    copies += [multiply(1, 0, own_turned.at[1]), multiply(1, 1, turned.at[1])]
+    for copy in copies:
+        copy.wait()
+
+
+def fourier_call(own_turned, other, table_north, turns, limits, table, half_width, fields):
     shape = (2, 2 * fields, half_width)
     return pl.pallas_call(
         functools.partial(fourier_kernel, fields),
         out_shape=jax.ShapeDtypeStruct(shape, jnp.bfloat16),
-        in_specs=[pl.BlockSpec(memory_space=pl.ANY)] * 5,
+        in_specs=[pl.BlockSpec(memory_space=pltpu.VMEM)] * 5
+        + [pl.BlockSpec(memory_space=pl.ANY)],
         out_specs=pl.BlockSpec(memory_space=pl.ANY),
         scratch_shapes=[
-            pltpu.SMEM((2,), jnp.int32),
-            pltpu.VMEM((2,) + own.shape, jnp.bfloat16),
-            pltpu.VMEM(table.shape, jnp.bfloat16),
-            pltpu.VMEM(turns.shape, jnp.float32),
-            pltpu.VMEM((2, 2048, 128), jnp.float32),
-            pltpu.VMEM((2, 2, 1024, 128), jnp.bfloat16),
-            pltpu.VMEM((2, 2, 128, 1024), jnp.float32),
-            turned,
-            turned,
+            pltpu.VMEM(table_north.shape, jnp.bfloat16),
+            pltpu.VMEM((2048, 128), jnp.float32),
+            pltpu.VMEM((2, 1024, 128), jnp.bfloat16),
+            pltpu.VMEM((2, 128, 1024), jnp.float32),
+            pltpu.VMEM(own_turned.shape, jnp.bfloat16),
             pltpu.VMEM(shape, jnp.bfloat16),
-            pltpu.SemaphoreType.DMA((8,)),
-        ],
-        compiler_params=pltpu.CompilerParams(vmem_limit_bytes=58 << 20),
+            pltpu.SemaphoreType.DMA((5,)),
+        ],
+        compiler_params=pltpu.CompilerParams(vmem_limit_bytes=VMEM),
         name="fourier",
-    )(lengths, own, other, table, turns)
+    )(own_turned, other, table_north, turns, limits, table)
 
 
 def on_device(spectra, legendre, wave_slots, row_length):
@@ -337,7 +352,10 @@
     table, turns = table_call(scalars, waves, half_width)
     arrived, table, turns = lax.optimization_barrier((arrived, table, turns))
     other = lax.ppermute(arrived, "lev", [(0, 1), (1, 0)])
-    return fourier_call(row_length, arrived, other, table, turns, half_width, fields)
+    own_turned, table_north, turns, limits = own_call(row_length, arrived, table, turns, fields)
+    return fourier_call(
+        own_turned, other, table_north, turns, limits, table, half_width, fields
+    )
 
 
 def solution(mesh):

time: 53.9 us -> 51.3 us (0.952)
  local copies, waits for them, and re-layouts: 4.04 us -> 2.55 us
  waiting for transfers between devices: 12 us -> 11.1 us
    pallas_call x1, Pallas kernels: 8.24 us -> 5.14 us  [fourier_call(): pl.pallas_call(functools.partial(fourier_kernel, fields), out_shape=jax.S...]
    pallas_call x0 -> x1, Pallas kernels: none -> 2.8 us  [own_call(): pl.pallas_call(own_kernel, out_shape=[jax.ShapeDtypeStruct((2, PIECES * f...]
    ppermute x1, waiting for transfers between devices: 1.54 us -> 0.01 us  [on_device(): other = lax.ppermute(arrived, 'lev', [(0, 1), (1, 0)])]
    unnamed x13 -> x7, local copies, waits for them, and re-layouts: 3.84 us -> 2.36 us
    all_to_all x1, waiting for transfers between devices: 10.5 us -> 11.1 us  [on_device(): lax.all_to_all(sent, 'wave', split_axis=0, concat_axis=0, tiled=True)]
  transfers between devices with their start and end apart: 2 -> 2, of which waited for: 2 -> 1; matrix products, arithmetic and copies ran while one was open for 1% -> 1% of each run, Pallas kernels for 10% -> 16%
where the time goes in v3:
time: 51.3 us; the launch traced here: 51.1 us
  starting transfers between devices  18.9 us (37%)
  Pallas kernels  18.4 us (36%)
  waiting for transfers between devices  11.1 us (22%)
  local copies, waits for them, and re-layouts  2.55 us (5%)
    all_to_all x1, starting transfers between devices, on_device(): lax.all_to_all(sent, 'wave', split_axis=0, concat_axis=0, tiled=True)  16.3 us
    all_to_all x1, waiting for transfers between devices, on_device(): lax.all_to_all(sent, 'wave', split_axis=0, concat_axis=0, tiled=True)  11.1 us
    pallas_call x1, Pallas kernels, table_call(): pl.pallas_call(functools.partial(table_kernel, half_width), out_shape=[ja...  5.3 us
    pallas_call x1, Pallas kernels, fourier_call(): pl.pallas_call(functools.partial(fourier_kernel, fields), out_shape=jax.S...  5.14 us
    pallas_call x1, Pallas kernels, legendre_call(): pl.pallas_call(legendre_kernel, out_shape=jax.ShapeDtypeStruct((128, 16,...  5.13 us
    pallas_call x1, Pallas kernels, own_call(): pl.pallas_call(own_kernel, out_shape=[jax.ShapeDtypeStruct((2, PIECES * f...  2.8 us
    ppermute x1, starting transfers between devices, on_device(): other = lax.ppermute(arrived, 'lev', [(0, 1), (1, 0)])  2.53 us
    unnamed x7, local copies, waits for them, and re-layouts  2.36 us
  transfers between devices with their start and end apart: 2, of which 1 were waited for; matrix products, arithmetic and copies ran while one was open for 1% of the time, Pallas kernels for 16%

profile of v3, /device:TPU:1, one launch (start us, length us, event | category | flops | bytes accessed | tf_op | source)
XLA Modules:
  0.0 51.1 jit_solution(18046616197981451285)
XLA Ops:
  0.0 0.0 copy-start.2
  0.0 0.0 copy-start.1
  0.0 5.1 %legendre.2 = bf16[128,16,128]{2,1,0:T(8,128)(2,1)} custom-call(s32[1280]{0:T(1024)} %waves_ref.1, bf16[10,128,1280]{2,1,0:T(8,128)(2,1)} %legendre.3, bf16[10,96,1280]{2,1,0:T(8,128)(2,1)} %spectra.1), custom_call_target="tpu_custom_call" | custom-call | tf_op jit(solution)/shard_map/legendre/pallas_call | solution.py:80
  5.1 16.3 %all-to-all-start = ((bf16[128,16,128]{2,1,0:T(8,128)(2,1)}), bf16[128,16,128]{2,1,0:T(8,128)(2,1)S(1)}, u32[]{:S(2)}, u32[]{:S(2)}) async-start(bf16[128,16,128]{2,1,0:T(8,128)(2,1)} %legendre.2), calls=%async_computation | async-start | bytes 1048576 | tf_op jit(solution)/shard_map/all_to_all | solution.py:351
  21.5 0.0 copy-done.2
  21.5 0.1 reshape.6
  21.7 0.1 copy.5
  21.7 0.0 copy-done.1
  21.7 0.1 pad_add_fusion.scalars
  21.8 5.3 %tables.1 = (bf16[2,528,2560]{2,1,0:T(8,128)(2,1)S(1)}, f32[2,16,1280]{2,1,0:T(8,128)S(1)}) custom-call(s32[3]{0:T(128)S(1)} %pad_add_fusion.scalars, s32[1,1280]{1,0:T(1,128)S(1)} %bitcast.7), custom_call_target="tpu_custom_call" | custom-call | flops 20000000 | bytes 6000000 | tf_op jit(solution)/shard_map/tables/pallas_call | solution.py:139
  27.1 0.0 copy-start
  27.1 2.3 %copy-done = bf16[2,528,2560]{2,1,0:T(8,128)(2,1)} copy-done((bf16[2,528,2560]{2,1,0:T(8,128)(2,1)}, bf16[2,528,2560]{2,1,0:T(8,128)(2,1)S(1)}, u32[]{:S(2)}) %copy-start) | copy-done | bytes 5406744
  29.5 11.1 %all-to-all-done.own = bf16[128,16,128]{2,1,0:T(8,128)(2,1)S(1)} async-done(((bf16[128,16,128]{2,1,0:T(8,128)(2,1)}), bf16[128,16,128]{2,1,0:T(8,128)(2,1)S(1)}, u32[]{:S(2)}, u32[]{:S(2)}) %all-to-all-start) | async-done | bytes 524320 | tf_op jit(solution)/shard_map/all_to_all | solution.py:351
  40.6 2.5 %collective-permute-start = (bf16[128,16,128]{2,1,0:T(8,128)(2,1)S(1)}, bf16[128,16,128]{2,1,0:T(8,128)(2,1)S(1)}, u32[]{:S(2)}, u32[]{:S(2)}) collective-permute-start(bf16[128,16,128]{2,1,0:T(8,128)(2,1)S(1)} %all-to-all-done.own), channel_id=1, source_target_pairs={{0,1},{1,0},{2,3},{3,2},{4,5},{5,4},{6,7},{7,6},{8,9},{9,8},{10,11... | collective-permute-start | bytes 1572872 | tf_op jit(solution)/shard_map/ppermute | solution.py:354
  43.1 2.8 %own.1 = (bf16[2,240,2560]{2,1,0:T(8,128)(2,1)S(1)}, bf16[528,2560]{1,0:T(8,128)(2,1)S(1)}, f32[2,16,1280]{2,1,0:T(8,128)S(1)}, s32[16,512]{1,0:T(8,128)S(1)}) custom-call(s32[2]{0:T(128)S(1)} %copy-done.1, bf16[128,16,128]{2,1,0:T(8,128)(2,1)S(1)} %all-to-all-done.own, bf16[2,528,2560]{2,1,0:T(8,128)(2,1)} %copy-done, ...), custom_call_target="tpu_custom_call" | custom-call | flops 40000000 | bytes 6000000 | tf_op jit(solution)/shard_map/own/pallas_call | solution.py:219
  46.0 0.0 collective-permute-done.other
  46.0 5.1 %fourier.1 = bf16[2,96,2568]{2,1,0:T(8,128)(2,1)} custom-call(bf16[2,240,2560]{2,1,0:T(8,128)(2,1)S(1)} %get-tuple-element.19.own_turned, bf16[128,16,128]{2,1,0:T(8,128)(2,1)S(1)} %collective-permute-done.other, bf16[528,2560]{1,0:T(8,128)(2,1)S(1)} %get-tuple-element.20.table_north, f32[2,16,1280]{2,1,0:T(8,128)S(1)} %get-tuple-element.21.turns, ...), custom_call_target="tpu_custom_call" | custom-call | tf_op jit(solution)/shard_map/fourier/pallas_call | solution.py:322
  (1 shorter events, 0.0 us)
Async XLA Ops:
  0.0 21.5 %copy-start.2 = (s32[1280]{0:T(1024)S(1)}, s32[1280]{0:T(1024)}, u32[]{:S(2)}) copy-start(s32[1280]{0:T(1024)} %waves_ref.1) | copy-start | bytes 15364
  0.0 21.7 %copy-start.1 = (s32[2]{0:T(128)S(1)}, s32[2]{0:T(128)}, u32[]{:S(2)}) copy-start(s32[2]{0:T(128)} %lengths.1) | copy-start | bytes 28
  5.1 35.5 %all-to-all-start = ((bf16[128,16,128]{2,1,0:T(8,128)(2,1)}), bf16[128,16,128]{2,1,0:T(8,128)(2,1)S(1)}, u32[]{:S(2)}, u32[]{:S(2)}) async-start(bf16[128,16,128]{2,1,0:T(8,128)(2,1)} %legendre.2), calls=%async_computation | async-start | bytes 1048576 | tf_op jit(solution)/shard_map/all_to_all | solution.py:351
  27.1 2.3 %copy-start = (bf16[2,528,2560]{2,1,0:T(8,128)(2,1)}, bf16[2,528,2560]{2,1,0:T(8,128)(2,1)S(1)}, u32[]{:S(2)}) copy-start(bf16[2,528,2560]{2,1,0:T(8,128)(2,1)S(1)} %get-tuple-element.17.table_ref) | copy-start | bytes 16220164
  40.6 5.3 %collective-permute-start = (bf16[128,16,128]{2,1,0:T(8,128)(2,1)S(1)}, bf16[128,16,128]{2,1,0:T(8,128)(2,1)S(1)}, u32[]{:S(2)}, u32[]{:S(2)}) collective-permute-start(bf16[128,16,128]{2,1,0:T(8,128)(2,1)S(1)} %all-to-all-done.own), channel_id=1, source_target_pairs={{0,1},{1,0},{2,3},{3,2},{4,5},{5,4},{6,7},{7,6},{8,9},{9,8},{10,11... | collective-permute-start | bytes 1572872 | tf_op jit(solution)/shard_map/ppermute | solution.py:354

commit v4 on v3

--- a/solution.py
+++ b/solution.py
@@ -3,6 +3,7 @@
 
 import jax
 import jax.numpy as jnp
+import numpy as np
 from jax import lax
 from jax.experimental import pallas as pl
 from jax.experimental.pallas import tpu as pltpu
@@ -15,7 +16,27 @@
 CHUNK = 256
 
 
-def legendre_kernel(waves_ref, legendre, spectra, sent, waves, tables, spectrum, sums, rows, sems, wave_sem):
+def exchange_order():
+    x, y, z = np.meshgrid(np.arange(4), np.arange(4), np.arange(8), indexing="ij")
+    hops = np.minimum(x, 4 - x) + np.minimum(y, 4 - y) + np.minimum(z, 8 - z)
+    return np.argsort(-hops.reshape(-1), kind="stable")
+
+
+def legendre_kernel(
+    waves_ref,
+    order_ref,
+    legendre,
+    spectra,
+    sent,
+    waves,
+    order,
+    tables,
+    spectrum,
+    sums,
+    rows,
+    sems,
+    extra,
+):
     slots, columns, degrees = spectrum.shape
     lats = tables.shape[1]
     steps = degrees // CHUNK + 1
@@ -26,16 +47,15 @@
         )
         for slot in range(slots)
     ]
-    fetch = pltpu.make_async_copy(waves_ref, waves, wave_sem)
+    fetch = pltpu.make_async_copy(waves_ref, waves, extra.at[0])
     fetch.start()
+    fetch_order = pltpu.make_async_copy(order_ref, order, extra.at[1])
+    fetch_order.start()
     for both in copies:
         for copy in both:
             copy.start()
     first = lax.axis_index("wave") * slots
     sums[...] = jnp.zeros_like(sums)
-    i = lax.broadcasted_iota(jnp.int32, (lats, lats), 0)
-    j = lax.broadcasted_iota(jnp.int32, (lats, lats), 1)
-    same = jnp.where(i == j, 1.0, 0.0).astype(jnp.bfloat16)
     fetch.wait()
     for pair in range(slots // 2):
         for slot in (2 * pair, 2 * pair + 1):
@@ -60,40 +80,44 @@
                 preferred_element_type=jnp.float32,
             )
             at = pl.ds(pl.multiple_of(slot * columns, 32), columns)
-            sums[0, at, :] += both[0:columns]
-            sums[1, at, :] += both[columns:]
+            sums[at, 0:lats] += both[0:columns]
+            sums[at, lats:] += both[columns:]
+        if pair == 0:
+            fetch_order.wait()
         done = [pair * 2 * columns // 128, (pair + 1) * 2 * columns // 128]
         for part in range(done[0], done[1] if pair < slots // 2 - 1 else 8):
-            for side in (0, 1):
-                rows[pl.ds(side * 1024 + part, lats, stride=8), :] = lax.dot_general(
-                    same,
-                    sums[side, part * 128 : part * 128 + 128].astype(jnp.bfloat16),
-                    NT,
-                    preferred_element_type=jnp.float32,
-                )
+            rows[pl.ds(part, 2 * lats, stride=8), :] = lax.dot_general(
+                order[...],
+                sums[part * 128 : part * 128 + 128].astype(jnp.bfloat16),
+                NT,
+                preferred_element_type=jnp.float32,
+            )
     sent[...] = rows[...].astype(jnp.bfloat16).reshape(sent.shape)
 
 
 def legendre_call(waves, legendre, spectra):
     slots, lats, degrees = legendre.shape
     columns = spectra.shape[1]
+    lines = (2 * exchange_order()[:, None] + np.arange(2)).reshape(-1)
+    order = jnp.asarray(lines[:, None] == np.arange(2 * lats), jnp.bfloat16)
     return pl.pallas_call(
         legendre_kernel,
         out_shape=jax.ShapeDtypeStruct((128, 16, 128), jnp.bfloat16),
-        in_specs=[pl.BlockSpec(memory_space=pl.ANY)] * 3,
+        in_specs=[pl.BlockSpec(memory_space=pl.ANY)] * 4,
         out_specs=pl.BlockSpec(memory_space=pltpu.VMEM),
         scratch_shapes=[
             pltpu.SMEM(waves.shape, jnp.int32),
+            pltpu.VMEM(order.shape, jnp.bfloat16),
             pltpu.VMEM((slots, lats, degrees), jnp.bfloat16),
             pltpu.VMEM((slots, columns, degrees), jnp.bfloat16),
-            pltpu.VMEM((2, 1024, lats), jnp.float32),
+            pltpu.VMEM((1024, 2 * lats), jnp.float32),
             pltpu.VMEM((2048, 128), jnp.float32),
             pltpu.SemaphoreType.DMA((slots, 2)),
-            pltpu.SemaphoreType.DMA,
+            pltpu.SemaphoreType.DMA((2,)),
         ],
         compiler_params=pltpu.CompilerParams(vmem_limit_bytes=60 << 20),
         name="legendre",
-    )(waves, legendre, spectra)
+    )(waves, order, legendre, spectra)
 
 
 def circle(waves, starts, length):
@@ -118,7 +142,8 @@
     weight = jnp.where(wave <= (row_length - 1) // 2, weight, 0.0)
     eight = lax.broadcasted_iota(jnp.int32, (8, total), 0)
     cos_a, sin_a = circle(waves, (eight * BLOCK + start).astype(jnp.float32), length)
-    turns[0, 0:8] = cos_a * weight
+    last = lax.broadcasted_iota(jnp.int32, (8, total), 0) == 7
+    turns[0, 0:8] = jnp.where(last, length, cos_a * weight)
     turns[0, 8:16] = sin_a * weight
     coarse = lax.broadcasted_iota(jnp.int32, coarse_cos.shape, 0) * 16
     coarse_cos[...], coarse_sin[...] = circle(waves, coarse.astype(jnp.float32), length)
@@ -194,7 +219,7 @@
 
 
 def own_kernel(
-    lengths, own, table_ref, turns_ref, turned, table, turns, limits, rows, parts, bands, sems
+    own, table_ref, turns_ref, turned, table, turns, rows, parts, bands, sems
 ):
     fetch = [
         pltpu.make_async_copy(turns_ref, turns, sems.at[0]),
@@ -202,8 +227,6 @@
     ]
     for copy in fetch:
         copy.start()
-    for lat in (0, 1):
-        limits[8 * lat : 8 * lat + 8] = jnp.full((8, BLOCK), lengths[lat], jnp.int32)
     unpack(own, rows, parts, (bands.at[0], bands.at[1]))
     fetch[0].wait()
 
@@ -215,22 +238,20 @@
     fetch[1].wait()
 
 
-def own_call(lengths, own, table, turns, fields):
+def own_call(own, table, turns, fields):
     return pl.pallas_call(
         own_kernel,
         out_shape=[
             jax.ShapeDtypeStruct((2, PIECES * fields, table.shape[2]), jnp.bfloat16),
             jax.ShapeDtypeStruct(table.shape[1:], jnp.bfloat16),
             jax.ShapeDtypeStruct(turns.shape, jnp.float32),
-            jax.ShapeDtypeStruct((16, BLOCK), jnp.int32),
         ],
         in_specs=[
-            pl.BlockSpec(memory_space=pltpu.SMEM),
             pl.BlockSpec(memory_space=pltpu.VMEM),
             pl.BlockSpec(memory_space=pl.ANY),
             pl.BlockSpec(memory_space=pl.ANY),
         ],
-        out_specs=[pl.BlockSpec(memory_space=pltpu.VMEM)] * 4,
+        out_specs=[pl.BlockSpec(memory_space=pltpu.VMEM)] * 3,
         scratch_shapes=[
             pltpu.VMEM((2048, 128), jnp.float32),
             pltpu.VMEM((2, 1024, 128), jnp.bfloat16),
@@ -242,7 +263,7 @@
             flops=40_000_000, bytes_accessed=6_000_000, transcendentals=0
         ),
         name="own",
-    )(lengths, own, table, turns)
+    )(own, table, turns)
 
 
 def fourier_kernel(
@@ -251,7 +272,6 @@
     other,
     table_north,
     turns,
-    limits,
     table_ref,
     out_ref,
     table_south,
@@ -284,7 +304,7 @@
             beside()
         level = pl.ds(pl.multiple_of((number ^ lev) * fields, 16), fields)
         column = lax.broadcasted_iota(jnp.int32, (1, BLOCK), 1) + start
-        limit = limits[8 * lat : 8 * lat + 1]
+        limit = turns[lat, 7:8, 0:BLOCK].astype(jnp.int32)
         for piece in range(PIECES):
             out[lat, level, piece * BLOCK : piece * BLOCK + BLOCK] = jnp.where(
                 column + piece * BLOCK < limit, values[piece * fields : piece * fields + fields], 0.0
@@ -317,12 +337,12 @@
         copy.wait()
 
 
-def fourier_call(own_turned, other, table_north, turns, limits, table, half_width, fields):
+def fourier_call(own_turned, other, table_north, turns, table, half_width, fields):
     shape = (2, 2 * fields, half_width)
     return pl.pallas_call(
         functools.partial(fourier_kernel, fields),
         out_shape=jax.ShapeDtypeStruct(shape, jnp.bfloat16),
-        in_specs=[pl.BlockSpec(memory_space=pltpu.VMEM)] * 5
+        in_specs=[pl.BlockSpec(memory_space=pltpu.VMEM)] * 4
         + [pl.BlockSpec(memory_space=pl.ANY)],
         out_specs=pl.BlockSpec(memory_space=pl.ANY),
         scratch_shapes=[
@@ -336,7 +356,7 @@
         ],
         compiler_params=pltpu.CompilerParams(vmem_limit_bytes=VMEM),
         name="fourier",
-    )(own_turned, other, table_north, turns, limits, table)
+    )(own_turned, other, table_north, turns, table)
 
 
 def on_device(spectra, legendre, wave_slots, row_length):
@@ -346,16 +366,22 @@
     half_width = (4 * total + 16) // 2
     lev = lax.axis_index("lev").astype(jnp.int32)
     scalars = jnp.concatenate([row_length, lev[None]])
-    waves = wave_slots.reshape(total // slots, slots).T.reshape(1, total)
+    order = exchange_order()
+    waves = wave_slots.reshape(total // slots, slots)[order].T.reshape(1, total)
     sent = legendre_call(wave_slots, legendre, spectra)
-    arrived = lax.all_to_all(sent, "wave", split_axis=0, concat_axis=0, tiled=True)
+    arrived = lax.all_to_all(
+        sent,
+        "wave",
+        split_axis=0,
+        concat_axis=0,
+        axis_index_groups=[[int(chip) for chip in order]],
+        tiled=True,
+    )
     table, turns = table_call(scalars, waves, half_width)
     arrived, table, turns = lax.optimization_barrier((arrived, table, turns))
     other = lax.ppermute(arrived, "lev", [(0, 1), (1, 0)])
-    own_turned, table_north, turns, limits = own_call(row_length, arrived, table, turns, fields)
-    return fourier_call(
-        own_turned, other, table_north, turns, limits, table, half_width, fields
-    )
+    own_turned, table_north, turns = own_call(arrived, table, turns, fields)
+    return fourier_call(own_turned, other, table_north, turns, table, half_width, fields)
 
 
 def solution(mesh):

time: 51.3 us -> 45.2 us (0.88)
  waiting for transfers between devices: 11.1 us -> 1.7 us
  starting transfers between devices: 18.9 us -> 21 us
  local copies, waits for them, and re-layouts: 2.55 us -> 3.22 us
    all_to_all x1, waiting for transfers between devices: 11.1 us -> 1.7 us  [on_device(): lax.all_to_all(sent, 'wave', split_axis=0, concat_axis=0, axis_index_grou...]
    all_to_all x1, starting transfers between devices: 16.3 us -> 19.2 us  [on_device(): lax.all_to_all(sent, 'wave', split_axis=0, concat_axis=0, axis_index_grou...]
    pallas_call x1, Pallas kernels: 5.13 us -> 6.3 us  [legendre_call(): pl.pallas_call(legendre_kernel, out_shape=jax.ShapeDtypeStruct((128, 16,...]
    ppermute x1, starting transfers between devices: 2.53 us -> 1.74 us  [on_device(): other = lax.ppermute(arrived, 'lev', [(0, 1), (1, 0)])]
    gather x0 -> x1, local copies, waits for them, and re-layouts: none -> 0.65 us  [on_device(): waves = wave_slots.reshape(total // slots, slots)[order].T.reshape(1, total)]
    pallas_call x1, Pallas kernels: 2.8 us -> 2.19 us  [own_call(): pl.pallas_call(own_kernel, out_shape=[jax.ShapeDtypeStruct((2, PIECES * f...]
    unnamed x7 -> x9, local copies, waits for them, and re-layouts: 2.36 us -> 2.38 us
  transfers between devices with their start and end apart: 2 -> 2, of which waited for: 1 -> 1; matrix products, arithmetic and copies ran while one was open for 1% -> 2% of each run, Pallas kernels for 16% -> 17%
where the time goes in v4:
time: 45.2 us; the launch traced here: 45 us
  starting transfers between devices  21 us (46%)
  Pallas kernels  18.9 us (42%)
  local copies, waits for them, and re-layouts  3.22 us (7%)
  waiting for transfers between devices  1.7 us (4%)
    all_to_all x1, starting transfers between devices, on_device(): lax.all_to_all(sent, 'wave', split_axis=0, concat_axis=0, axis_index_grou...  19.2 us
    pallas_call x1, Pallas kernels, legendre_call(): pl.pallas_call(legendre_kernel, out_shape=jax.ShapeDtypeStruct((128, 16,...  6.3 us
    pallas_call x1, Pallas kernels, table_call(): pl.pallas_call(functools.partial(table_kernel, half_width), out_shape=[ja...  5.3 us
    pallas_call x1, Pallas kernels, fourier_call(): pl.pallas_call(functools.partial(fourier_kernel, fields), out_shape=jax.S...  5.11 us
    unnamed x9, local copies, waits for them, and re-layouts  2.38 us
    pallas_call x1, Pallas kernels, own_call(): pl.pallas_call(own_kernel, out_shape=[jax.ShapeDtypeStruct((2, PIECES * f...  2.19 us
    ppermute x1, starting transfers between devices, on_device(): other = lax.ppermute(arrived, 'lev', [(0, 1), (1, 0)])  1.74 us
    all_to_all x1, waiting for transfers between devices, on_device(): lax.all_to_all(sent, 'wave', split_axis=0, concat_axis=0, axis_index_grou...  1.7 us
  transfers between devices with their start and end apart: 2, of which 1 were waited for; matrix products, arithmetic and copies ran while one was open for 2% of the time, Pallas kernels for 17%

profile of v4, /device:TPU:1, one launch (start us, length us, event | category | flops | bytes accessed | tf_op | source)
XLA Modules:
  0.0 45.0 jit_solution(8753926769332725106)
XLA Ops:
  0.0 0.0 copy-start.2
  0.0 0.0 copy-start.1
  0.0 0.0 copy-start.3
  0.0 6.3 %legendre.2 = bf16[128,16,128]{2,1,0:T(8,128)(2,1)} custom-call(s32[1280]{0:T(1024)} %waves_ref.1, bf16[256,256]{1,0:T(8,128)(2,1)} %constant.14.clone.order_ref, bf16[10,128,1280]{2,1,0:T(8,128)(2,1)} %legendre.3, bf16[10,96,1280]{2,1,0:T(8,128)(2,1)} %spectra.1), custom_call_target="tpu_custom_call" | custom-call | tf_op jit(solution)/shard_map/legendre/pallas_call | solution.py:103
  6.3 19.2 %all-to-all-start = ((bf16[128,16,128]{2,1,0:T(8,128)(2,1)}), bf16[128,16,128]{2,1,0:T(8,128)(2,1)S(1)}, u32[]{:S(2)}, u32[]{:S(2)}) async-start(bf16[128,16,128]{2,1,0:T(8,128)(2,1)} %legendre.2), calls=%async_computation | async-start | bytes 1048576 | tf_op jit(solution)/shard_map/all_to_all | solution.py:372
  25.5 0.0 copy-done.1
  25.6 0.1 reshape.6
  25.7 0.0 copy-done.2
  25.7 0.6 %gather_fusion = s32[128,10]{1,0:T(8,128)S(1)} fusion(s32[128,10]{1,0:T(8,128)S(1)} %reshape.6, s32[1024]{0:T(1024)S(1)} %pad_clamp_fusion), kind=kCustom, calls=%fused_computation | custom fusion | bytes 10752 | tf_op jit(solution)/shard_map/gather | solution.py:370
  26.4 0.1 copy.9
  26.4 0.0 copy-done.3
  26.5 0.1 pad_add_fusion.scalars
  26.5 5.3 %tables.1 = (bf16[2,528,2560]{2,1,0:T(8,128)(2,1)S(1)}, f32[2,16,1280]{2,1,0:T(8,128)S(1)}) custom-call(s32[3]{0:T(128)S(1)} %pad_add_fusion.scalars, s32[1,1280]{1,0:T(1,128)S(1)} %bitcast.7), custom_call_target="tpu_custom_call" | custom-call | flops 20000000 | bytes 6000000 | tf_op jit(solution)/shard_map/tables/pallas_call | solution.py:164
  31.8 0.0 copy-start
  31.9 2.3 %copy-done = bf16[2,528,2560]{2,1,0:T(8,128)(2,1)} copy-done((bf16[2,528,2560]{2,1,0:T(8,128)(2,1)}, bf16[2,528,2560]{2,1,0:T(8,128)(2,1)S(1)}, u32[]{:S(2)}) %copy-start) | copy-done | bytes 5406744
  34.2 1.7 %all-to-all-done.own = bf16[128,16,128]{2,1,0:T(8,128)(2,1)S(1)} async-done(((bf16[128,16,128]{2,1,0:T(8,128)(2,1)}), bf16[128,16,128]{2,1,0:T(8,128)(2,1)S(1)}, u32[]{:S(2)}, u32[]{:S(2)}) %all-to-all-start) | async-done | bytes 524320 | tf_op jit(solution)/shard_map/all_to_all | solution.py:372
  35.9 1.7 %collective-permute-start = (bf16[128,16,128]{2,1,0:T(8,128)(2,1)S(1)}, bf16[128,16,128]{2,1,0:T(8,128)(2,1)S(1)}, u32[]{:S(2)}, u32[]{:S(2)}) collective-permute-start(bf16[128,16,128]{2,1,0:T(8,128)(2,1)S(1)} %all-to-all-done.own), channel_id=1, source_target_pairs={{0,1},{1,0},{2,3},{3,2},{4,5},{5,4},{6,7},{7,6},{8,9},{9,8},{10,11... | collective-permute-start | bytes 1572872 | tf_op jit(solution)/shard_map/ppermute | solution.py:382
  37.6 2.2 %own.1 = (bf16[2,240,2560]{2,1,0:T(8,128)(2,1)S(1)}, bf16[528,2560]{1,0:T(8,128)(2,1)S(1)}, f32[2,16,1280]{2,1,0:T(8,128)S(1)}) custom-call(bf16[128,16,128]{2,1,0:T(8,128)(2,1)S(1)} %all-to-all-done.own, bf16[2,528,2560]{2,1,0:T(8,128)(2,1)} %copy-done, f32[2,16,1280]{2,1,0:T(8,128)S(1)} %get-tuple-element.17.turns_ref), custom_call_target="tpu_custom_call" | custom-call | flops 40000000 | bytes 6000000 | tf_op jit(solution)/shard_map/own/pallas_call | solution.py:242
  39.8 0.0 collective-permute-done.other
  39.9 5.1 %fourier.1 = bf16[2,96,2568]{2,1,0:T(8,128)(2,1)} custom-call(bf16[2,240,2560]{2,1,0:T(8,128)(2,1)S(1)} %get-tuple-element.18.own_turned, bf16[128,16,128]{2,1,0:T(8,128)(2,1)S(1)} %collective-permute-done.other, bf16[528,2560]{1,0:T(8,128)(2,1)S(1)} %get-tuple-element.19.table_north, f32[2,16,1280]{2,1,0:T(8,128)S(1)} %get-tuple-element.20.turns, ...), custom_call_target="tpu_custom_call" | custom-call | tf_op jit(solution)/shard_map/fourier/pallas_call | solution.py:342
  (2 shorter events, 0.0 us)
Async XLA Ops:
  0.0 25.7 %copy-start.2 = (s32[128]{0:T(128)S(1)}, s32[128]{0:T(128)}, u32[]{:S(2)}) copy-start(s32[128]{0:T(128)} %constant.19) | copy-start | bytes 1540
  0.0 25.5 %copy-start.1 = (s32[1280]{0:T(1024)S(1)}, s32[1280]{0:T(1024)}, u32[]{:S(2)}) copy-start(s32[1280]{0:T(1024)} %waves_ref.1) | copy-start | bytes 15364
  0.0 26.4 %copy-start.3 = (s32[2]{0:T(128)S(1)}, s32[2]{0:T(128)}, u32[]{:S(2)}) copy-start(s32[2]{0:T(128)} %param.10) | copy-start | bytes 28
  6.3 29.6 %all-to-all-start = ((bf16[128,16,128]{2,1,0:T(8,128)(2,1)}), bf16[128,16,128]{2,1,0:T(8,128)(2,1)S(1)}, u32[]{:S(2)}, u32[]{:S(2)}) async-start(bf16[128,16,128]{2,1,0:T(8,128)(2,1)} %legendre.2), calls=%async_computation | async-start | bytes 1048576 | tf_op jit(solution)/shard_map/all_to_all | solution.py:372
  31.8 2.4 %copy-start = (bf16[2,528,2560]{2,1,0:T(8,128)(2,1)}, bf16[2,528,2560]{2,1,0:T(8,128)(2,1)S(1)}, u32[]{:S(2)}) copy-start(bf16[2,528,2560]{2,1,0:T(8,128)(2,1)S(1)} %get-tuple-element.16.table_ref) | copy-start | bytes 16220164
  35.9 3.9 %collective-permute-start = (bf16[128,16,128]{2,1,0:T(8,128)(2,1)S(1)}, bf16[128,16,128]{2,1,0:T(8,128)(2,1)S(1)}, u32[]{:S(2)}, u32[]{:S(2)}) collective-permute-start(bf16[128,16,128]{2,1,0:T(8,128)(2,1)S(1)} %all-to-all-done.own), channel_id=1, source_target_pairs={{0,1},{1,0},{2,3},{3,2},{4,5},{5,4},{6,7},{7,6},{8,9},{9,8},{10,11... | collective-permute-start | bytes 1572872 | tf_op jit(solution)/shard_map/ppermute | solution.py:382

commit v5 on v4

--- a/solution.py
+++ b/solution.py
@@ -82,16 +82,14 @@
             at = pl.ds(pl.multiple_of(slot * columns, 32), columns)
             sums[at, 0:lats] += both[0:columns]
             sums[at, lats:] += both[columns:]
-        if pair == 0:
-            fetch_order.wait()
-        done = [pair * 2 * columns // 128, (pair + 1) * 2 * columns // 128]
-        for part in range(done[0], done[1] if pair < slots // 2 - 1 else 8):
-            rows[pl.ds(part, 2 * lats, stride=8), :] = lax.dot_general(
-                order[...],
-                sums[part * 128 : part * 128 + 128].astype(jnp.bfloat16),
-                NT,
-                preferred_element_type=jnp.float32,
-            )
+    fetch_order.wait()
+    for part in range(8):
+        rows[pl.ds(part, 2 * lats, stride=8), :] = lax.dot_general(
+            order[...],
+            sums[part * 128 : part * 128 + 128].astype(jnp.bfloat16),
+            NT,
+            preferred_element_type=jnp.float32,
+        )
     sent[...] = rows[...].astype(jnp.bfloat16).reshape(sent.shape)
 
 

time: 45.2 us -> 43.5 us (0.962)
  Pallas kernels: 18.9 us -> 17.2 us
    pallas_call x1, Pallas kernels: 6.3 us -> 4.59 us  [legendre_call(): pl.pallas_call(legendre_kernel, out_shape=jax.ShapeDtypeStruct((128, 16,...]
where the time goes in v5:
time: 43.5 us; the launch traced here: 43.3 us
  starting transfers between devices  21 us (48%)
  Pallas kernels  17.2 us (40%)
  local copies, waits for them, and re-layouts  3.22 us (7%)
  waiting for transfers between devices  1.7 us (4%)
    all_to_all x1, starting transfers between devices, on_device(): lax.all_to_all(sent, 'wave', split_axis=0, concat_axis=0, axis_index_grou...  19.2 us
    pallas_call x1, Pallas kernels, table_call(): pl.pallas_call(functools.partial(table_kernel, half_width), out_shape=[ja...  5.3 us
    pallas_call x1, Pallas kernels, fourier_call(): pl.pallas_call(functools.partial(fourier_kernel, fields), out_shape=jax.S...  5.12 us
    pallas_call x1, Pallas kernels, legendre_call(): pl.pallas_call(legendre_kernel, out_shape=jax.ShapeDtypeStruct((128, 16,...  4.59 us
    unnamed x9, local copies, waits for them, and re-layouts  2.38 us
    pallas_call x1, Pallas kernels, own_call(): pl.pallas_call(own_kernel, out_shape=[jax.ShapeDtypeStruct((2, PIECES * f...  2.19 us
    ppermute x1, starting transfers between devices, on_device(): other = lax.ppermute(arrived, 'lev', [(0, 1), (1, 0)])  1.74 us
    all_to_all x1, waiting for transfers between devices, on_device(): lax.all_to_all(sent, 'wave', split_axis=0, concat_axis=0, axis_index_grou...  1.7 us
  transfers between devices with their start and end apart: 2, of which 1 were waited for; matrix products, arithmetic and copies ran while one was open for 2% of the time, Pallas kernels for 17%

profile of v5, /device:TPU:1, one launch (start us, length us, event | category | flops | bytes accessed | tf_op | source)
XLA Modules:
  0.0 43.3 jit_solution(14913152650695160495)
XLA Ops:
  0.0 0.0 copy-start.2
  0.0 0.0 copy-start.1
  0.0 0.0 copy-start.3
  0.0 4.6 %legendre.2 = bf16[128,16,128]{2,1,0:T(8,128)(2,1)} custom-call(s32[1280]{0:T(1024)} %waves_ref.1, bf16[256,256]{1,0:T(8,128)(2,1)} %constant.14.clone.order_ref, bf16[10,128,1280]{2,1,0:T(8,128)(2,1)} %legendre.3, bf16[10,96,1280]{2,1,0:T(8,128)(2,1)} %spectra.1), custom_call_target="tpu_custom_call" | custom-call | tf_op jit(solution)/shard_map/legendre/pallas_call | solution.py:101
  4.6 19.2 %all-to-all-start = ((bf16[128,16,128]{2,1,0:T(8,128)(2,1)}), bf16[128,16,128]{2,1,0:T(8,128)(2,1)S(1)}, u32[]{:S(2)}, u32[]{:S(2)}) async-start(bf16[128,16,128]{2,1,0:T(8,128)(2,1)} %legendre.2), calls=%async_computation | async-start | bytes 1048576 | tf_op jit(solution)/shard_map/all_to_all | solution.py:370
  23.8 0.0 copy-done.1
  23.8 0.1 reshape.6
  24.0 0.0 copy-done.2
  24.0 0.6 %gather_fusion = s32[128,10]{1,0:T(8,128)S(1)} fusion(s32[128,10]{1,0:T(8,128)S(1)} %reshape.6, s32[1024]{0:T(1024)S(1)} %pad_clamp_fusion), kind=kCustom, calls=%fused_computation | custom fusion | bytes 10752 | tf_op jit(solution)/shard_map/gather | solution.py:368
  24.7 0.1 copy.9
  24.7 0.0 copy-done.3
  24.7 0.1 pad_add_fusion.scalars
  24.8 5.3 %tables.1 = (bf16[2,528,2560]{2,1,0:T(8,128)(2,1)S(1)}, f32[2,16,1280]{2,1,0:T(8,128)S(1)}) custom-call(s32[3]{0:T(128)S(1)} %pad_add_fusion.scalars, s32[1,1280]{1,0:T(1,128)S(1)} %bitcast.7), custom_call_target="tpu_custom_call" | custom-call | flops 20000000 | bytes 6000000 | tf_op jit(solution)/shard_map/tables/pallas_call | solution.py:162
  30.1 0.0 copy-start
  30.1 2.3 %copy-done = bf16[2,528,2560]{2,1,0:T(8,128)(2,1)} copy-done((bf16[2,528,2560]{2,1,0:T(8,128)(2,1)}, bf16[2,528,2560]{2,1,0:T(8,128)(2,1)S(1)}, u32[]{:S(2)}) %copy-start) | copy-done | bytes 5406744
  32.5 1.7 %all-to-all-done.own = bf16[128,16,128]{2,1,0:T(8,128)(2,1)S(1)} async-done(((bf16[128,16,128]{2,1,0:T(8,128)(2,1)}), bf16[128,16,128]{2,1,0:T(8,128)(2,1)S(1)}, u32[]{:S(2)}, u32[]{:S(2)}) %all-to-all-start) | async-done | bytes 524320 | tf_op jit(solution)/shard_map/all_to_all | solution.py:370
  34.2 1.7 %collective-permute-start = (bf16[128,16,128]{2,1,0:T(8,128)(2,1)S(1)}, bf16[128,16,128]{2,1,0:T(8,128)(2,1)S(1)}, u32[]{:S(2)}, u32[]{:S(2)}) collective-permute-start(bf16[128,16,128]{2,1,0:T(8,128)(2,1)S(1)} %all-to-all-done.own), channel_id=1, source_target_pairs={{0,1},{1,0},{2,3},{3,2},{4,5},{5,4},{6,7},{7,6},{8,9},{9,8},{10,11... | collective-permute-start | bytes 1572872 | tf_op jit(solution)/shard_map/ppermute | solution.py:380
  35.9 2.2 %own.1 = (bf16[2,240,2560]{2,1,0:T(8,128)(2,1)S(1)}, bf16[528,2560]{1,0:T(8,128)(2,1)S(1)}, f32[2,16,1280]{2,1,0:T(8,128)S(1)}) custom-call(bf16[128,16,128]{2,1,0:T(8,128)(2,1)S(1)} %all-to-all-done.own, bf16[2,528,2560]{2,1,0:T(8,128)(2,1)} %copy-done, f32[2,16,1280]{2,1,0:T(8,128)S(1)} %get-tuple-element.17.turns_ref), custom_call_target="tpu_custom_call" | custom-call | flops 40000000 | bytes 6000000 | tf_op jit(solution)/shard_map/own/pallas_call | solution.py:240
  38.1 0.0 collective-permute-done.other
  38.2 5.1 %fourier.1 = bf16[2,96,2568]{2,1,0:T(8,128)(2,1)} custom-call(bf16[2,240,2560]{2,1,0:T(8,128)(2,1)S(1)} %get-tuple-element.18.own_turned, bf16[128,16,128]{2,1,0:T(8,128)(2,1)S(1)} %collective-permute-done.other, bf16[528,2560]{1,0:T(8,128)(2,1)S(1)} %get-tuple-element.19.table_north, f32[2,16,1280]{2,1,0:T(8,128)S(1)} %get-tuple-element.20.turns, ...), custom_call_target="tpu_custom_call" | custom-call | tf_op jit(solution)/shard_map/fourier/pallas_call | solution.py:340
  (2 shorter events, 0.0 us)
Async XLA Ops:
  0.0 24.0 %copy-start.2 = (s32[128]{0:T(128)S(1)}, s32[128]{0:T(128)}, u32[]{:S(2)}) copy-start(s32[128]{0:T(128)} %constant.19) | copy-start | bytes 1540
  0.0 23.8 %copy-start.1 = (s32[1280]{0:T(1024)S(1)}, s32[1280]{0:T(1024)}, u32[]{:S(2)}) copy-start(s32[1280]{0:T(1024)} %waves_ref.1) | copy-start | bytes 15364
  0.0 24.7 %copy-start.3 = (s32[2]{0:T(128)S(1)}, s32[2]{0:T(128)}, u32[]{:S(2)}) copy-start(s32[2]{0:T(128)} %param.10) | copy-start | bytes 28
  4.6 29.6 %all-to-all-start = ((bf16[128,16,128]{2,1,0:T(8,128)(2,1)}), bf16[128,16,128]{2,1,0:T(8,128)(2,1)S(1)}, u32[]{:S(2)}, u32[]{:S(2)}) async-start(bf16[128,16,128]{2,1,0:T(8,128)(2,1)} %legendre.2), calls=%async_computation | async-start | bytes 1048576 | tf_op jit(solution)/shard_map/all_to_all | solution.py:370
  30.1 2.4 %copy-start = (bf16[2,528,2560]{2,1,0:T(8,128)(2,1)}, bf16[2,528,2560]{2,1,0:T(8,128)(2,1)S(1)}, u32[]{:S(2)}) copy-start(bf16[2,528,2560]{2,1,0:T(8,128)(2,1)S(1)} %get-tuple-element.16.table_ref) | copy-start | bytes 16220164
  34.2 3.9 %collective-permute-start = (bf16[128,16,128]{2,1,0:T(8,128)(2,1)S(1)}, bf16[128,16,128]{2,1,0:T(8,128)(2,1)S(1)}, u32[]{:S(2)}, u32[]{:S(2)}) collective-permute-start(bf16[128,16,128]{2,1,0:T(8,128)(2,1)S(1)} %all-to-all-done.own), channel_id=1, source_target_pairs={{0,1},{1,0},{2,3},{3,2},{4,5},{5,4},{6,7},{7,6},{8,9},{9,8},{10,11... | collective-permute-start | bytes 1572872 | tf_op jit(solution)/shard_map/ppermute | solution.py:380

commit v6 on v5

--- a/solution.py
+++ b/solution.py
@@ -216,12 +216,24 @@
             turned[row : row + 16, behind] = (real * sin_a + imag * cos_a).astype(jnp.bfloat16)
 
 
+def table_copies(source, target, sems):
+    rows = target.shape[0] // 3
+    return [
+        pltpu.make_async_copy(
+            source.at[part * rows : part * rows + rows],
+            target.at[part * rows : part * rows + rows],
+            sems.at[part],
+        )
+        for part in range(3)
+    ]
+
+
 def own_kernel(
-    own, table_ref, turns_ref, turned, table, turns, rows, parts, bands, sems
+    own, table_ref, turns_ref, turned, table, turns, rows, parts, bands, sems, table_sems
 ):
     fetch = [
-        pltpu.make_async_copy(turns_ref, turns, sems.at[0]),
-        pltpu.make_async_copy(table_ref.at[0], table, sems.at[1]),
+        pltpu.make_async_copy(turns_ref, turns, sems),
+        *table_copies(table_ref.at[0], table, table_sems),
     ]
     for copy in fetch:
         copy.start()
@@ -233,7 +245,8 @@
         for lat in (0, 1):
             turn(bands.at[lat], turns, lat, slot, turned.at[lat])
 
-    fetch[1].wait()
+    for copy in fetch[1:]:
+        copy.wait()
 
 
 def own_call(own, table, turns, fields):
@@ -254,7 +267,8 @@
             pltpu.VMEM((2048, 128), jnp.float32),
             pltpu.VMEM((2, 1024, 128), jnp.bfloat16),
             pltpu.VMEM((2, 128, 1024), jnp.float32),
-            pltpu.SemaphoreType.DMA((2,)),
+            pltpu.SemaphoreType.DMA,
+            pltpu.SemaphoreType.DMA((3,)),
         ],
         compiler_params=pltpu.CompilerParams(vmem_limit_bytes=VMEM),
         cost_estimate=pl.CostEstimate(
@@ -279,13 +293,15 @@
     turned,
     out,
     sems,
+    table_sems,
 ):
     half_width = out.shape[2]
     slots = turns.shape[2] // 128
     lev = lax.axis_index("lev")
     start = lev * half_width
-    fetch = pltpu.make_async_copy(table_ref.at[1], table_south, sems.at[0])
-    fetch.start()
+    fetch = table_copies(table_ref.at[1], table_south, table_sems)
+    for copy in fetch:
+        copy.start()
 
     def multiply(lat, number, lines, beside=None):
         table = table_south if lat else table_north
@@ -312,7 +328,7 @@
             :, 0 : half_width - PIECES * BLOCK
         ].astype(jnp.bfloat16)
         copy = pltpu.make_async_copy(
-            out.at[lat, level], out_ref.at[lat, level], sems.at[1 + 2 * lat + number]
+            out.at[lat, level], out_ref.at[lat, level], sems.at[2 * lat + number]
         )
         copy.start()
         return copy
@@ -329,7 +345,8 @@
         multiply(0, 0, own_turned.at[0], open_other),
         multiply(0, 1, turned.at[0], lambda: turn_other(1)),
     ]
-    fetch.wait()
+    for copy in fetch:
+        copy.wait()
     copies += [multiply(1, 0, own_turned.at[1]), multiply(1, 1, turned.at[1])]
     for copy in copies:
         copy.wait()
@@ -350,7 +367,8 @@
             pltpu.VMEM((2, 128, 1024), jnp.float32),
             pltpu.VMEM(own_turned.shape, jnp.bfloat16),
             pltpu.VMEM(shape, jnp.bfloat16),
-            pltpu.SemaphoreType.DMA((5,)),
+            pltpu.SemaphoreType.DMA((4,)),
+            pltpu.SemaphoreType.DMA((3,)),
         ],
         compiler_params=pltpu.CompilerParams(vmem_limit_bytes=VMEM),
         name="fourier",

time: 43.5 us -> 44.5 us (1.023)
  Pallas kernels: 17.2 us -> 18.2 us
    pallas_call x1, Pallas kernels: 5.12 us -> 6.1 us  [fourier_call(): pl.pallas_call(functools.partial(fourier_kernel, fields), out_shape=jax.S...]
where the time goes in v6:
time: 44.5 us; the launch traced here: 44.2 us
  starting transfers between devices  21 us (47%)
  Pallas kernels  18.2 us (41%)
  local copies, waits for them, and re-layouts  3.22 us (7%)
  waiting for transfers between devices  1.7 us (4%)
    all_to_all x1, starting transfers between devices, on_device(): lax.all_to_all(sent, 'wave', split_axis=0, concat_axis=0, axis_index_grou...  19.2 us
    pallas_call x1, Pallas kernels, fourier_call(): pl.pallas_call(functools.partial(fourier_kernel, fields), out_shape=jax.S...  6.1 us
    pallas_call x1, Pallas kernels, table_call(): pl.pallas_call(functools.partial(table_kernel, half_width), out_shape=[ja...  5.3 us
    pallas_call x1, Pallas kernels, legendre_call(): pl.pallas_call(legendre_kernel, out_shape=jax.ShapeDtypeStruct((128, 16,...  4.6 us
    unnamed x9, local copies, waits for them, and re-layouts  2.38 us
    pallas_call x1, Pallas kernels, own_call(): pl.pallas_call(own_kernel, out_shape=[jax.ShapeDtypeStruct((2, PIECES * f...  2.18 us
    ppermute x1, starting transfers between devices, on_device(): other = lax.ppermute(arrived, 'lev', [(0, 1), (1, 0)])  1.74 us
    all_to_all x1, waiting for transfers between devices, on_device(): lax.all_to_all(sent, 'wave', split_axis=0, concat_axis=0, axis_index_grou...  1.7 us
  transfers between devices with their start and end apart: 2, of which 1 were waited for; matrix products, arithmetic and copies ran while one was open for 2% of the time, Pallas kernels for 17%

profile of v6, /device:TPU:1, one launch (start us, length us, event | category | flops | bytes accessed | tf_op | source)
XLA Modules:
  0.0 44.2 jit_solution(15388030441821486030)
XLA Ops:
  0.0 0.0 copy-start.2
  0.0 0.0 copy-start.1
  0.0 0.0 copy-start.3
  0.0 4.6 %legendre.2 = bf16[128,16,128]{2,1,0:T(8,128)(2,1)} custom-call(s32[1280]{0:T(1024)} %waves_ref.1, bf16[256,256]{1,0:T(8,128)(2,1)} %constant.14.clone.order_ref, bf16[10,128,1280]{2,1,0:T(8,128)(2,1)} %legendre.3, bf16[10,96,1280]{2,1,0:T(8,128)(2,1)} %spectra.1), custom_call_target="tpu_custom_call" | custom-call | tf_op jit(solution)/shard_map/legendre/pallas_call | solution.py:101
  4.6 19.2 %all-to-all-start = ((bf16[128,16,128]{2,1,0:T(8,128)(2,1)}), bf16[128,16,128]{2,1,0:T(8,128)(2,1)S(1)}, u32[]{:S(2)}, u32[]{:S(2)}) async-start(bf16[128,16,128]{2,1,0:T(8,128)(2,1)} %legendre.2), calls=%async_computation | async-start | bytes 1048576 | tf_op jit(solution)/shard_map/all_to_all | solution.py:388
  23.8 0.0 copy-done.1
  23.8 0.1 reshape.6
  24.0 0.0 copy-done.2
  24.0 0.6 %gather_fusion = s32[128,10]{1,0:T(8,128)S(1)} fusion(s32[128,10]{1,0:T(8,128)S(1)} %reshape.6, s32[1024]{0:T(1024)S(1)} %pad_clamp_fusion), kind=kCustom, calls=%fused_computation | custom fusion | bytes 10752 | tf_op jit(solution)/shard_map/gather | solution.py:386
  24.7 0.1 copy.9
  24.7 0.0 copy-done.3
  24.7 0.1 pad_add_fusion.scalars
  24.8 5.3 %tables.1 = (bf16[2,528,2560]{2,1,0:T(8,128)(2,1)S(1)}, f32[2,16,1280]{2,1,0:T(8,128)S(1)}) custom-call(s32[3]{0:T(128)S(1)} %pad_add_fusion.scalars, s32[1,1280]{1,0:T(1,128)S(1)} %bitcast.7), custom_call_target="tpu_custom_call" | custom-call | flops 20000000 | bytes 6000000 | tf_op jit(solution)/shard_map/tables/pallas_call | solution.py:162
  30.1 0.0 copy-start
  30.1 2.3 %copy-done = bf16[2,528,2560]{2,1,0:T(8,128)(2,1)} copy-done((bf16[2,528,2560]{2,1,0:T(8,128)(2,1)}, bf16[2,528,2560]{2,1,0:T(8,128)(2,1)S(1)}, u32[]{:S(2)}) %copy-start) | copy-done | bytes 5406744
  32.5 1.7 %all-to-all-done.own = bf16[128,16,128]{2,1,0:T(8,128)(2,1)S(1)} async-done(((bf16[128,16,128]{2,1,0:T(8,128)(2,1)}), bf16[128,16,128]{2,1,0:T(8,128)(2,1)S(1)}, u32[]{:S(2)}, u32[]{:S(2)}) %all-to-all-start) | async-done | bytes 524320 | tf_op jit(solution)/shard_map/all_to_all | solution.py:388
  34.2 1.7 %collective-permute-start = (bf16[128,16,128]{2,1,0:T(8,128)(2,1)S(1)}, bf16[128,16,128]{2,1,0:T(8,128)(2,1)S(1)}, u32[]{:S(2)}, u32[]{:S(2)}) collective-permute-start(bf16[128,16,128]{2,1,0:T(8,128)(2,1)S(1)} %all-to-all-done.own), channel_id=1, source_target_pairs={{0,1},{1,0},{2,3},{3,2},{4,5},{5,4},{6,7},{7,6},{8,9},{9,8},{10,11... | collective-permute-start | bytes 1572872 | tf_op jit(solution)/shard_map/ppermute | solution.py:398
  35.9 2.2 %own.1 = (bf16[2,240,2560]{2,1,0:T(8,128)(2,1)S(1)}, bf16[528,2560]{1,0:T(8,128)(2,1)S(1)}, f32[2,16,1280]{2,1,0:T(8,128)S(1)}) custom-call(bf16[128,16,128]{2,1,0:T(8,128)(2,1)S(1)} %all-to-all-done.own, bf16[2,528,2560]{2,1,0:T(8,128)(2,1)} %copy-done, f32[2,16,1280]{2,1,0:T(8,128)S(1)} %get-tuple-element.17.turns_ref), custom_call_target="tpu_custom_call" | custom-call | flops 40000000 | bytes 6000000 | tf_op jit(solution)/shard_map/own/pallas_call | solution.py:253
  38.1 0.0 collective-permute-done.other
  38.1 6.1 %fourier.1 = bf16[2,96,2568]{2,1,0:T(8,128)(2,1)} custom-call(bf16[2,240,2560]{2,1,0:T(8,128)(2,1)S(1)} %get-tuple-element.18.own_turned, bf16[128,16,128]{2,1,0:T(8,128)(2,1)S(1)} %collective-permute-done.other, bf16[528,2560]{1,0:T(8,128)(2,1)S(1)} %get-tuple-element.19.table_north, f32[2,16,1280]{2,1,0:T(8,128)S(1)} %get-tuple-element.20.turns, ...), custom_call_target="tpu_custom_call" | custom-call | tf_op jit(solution)/shard_map/fourier/pallas_call | solution.py:357
  (2 shorter events, 0.0 us)
Async XLA Ops:
  0.0 24.0 %copy-start.2 = (s32[128]{0:T(128)S(1)}, s32[128]{0:T(128)}, u32[]{:S(2)}) copy-start(s32[128]{0:T(128)} %constant.19) | copy-start | bytes 1540
  0.0 23.8 %copy-start.1 = (s32[1280]{0:T(1024)S(1)}, s32[1280]{0:T(1024)}, u32[]{:S(2)}) copy-start(s32[1280]{0:T(1024)} %waves_ref.1) | copy-start | bytes 15364
  0.0 24.7 %copy-start.3 = (s32[2]{0:T(128)S(1)}, s32[2]{0:T(128)}, u32[]{:S(2)}) copy-start(s32[2]{0:T(128)} %param.10) | copy-start | bytes 28
  4.6 29.6 %all-to-all-start = ((bf16[128,16,128]{2,1,0:T(8,128)(2,1)}), bf16[128,16,128]{2,1,0:T(8,128)(2,1)S(1)}, u32[]{:S(2)}, u32[]{:S(2)}) async-start(bf16[128,16,128]{2,1,0:T(8,128)(2,1)} %legendre.2), calls=%async_computation | async-start | bytes 1048576 | tf_op jit(solution)/shard_map/all_to_all | solution.py:388
  30.1 2.4 %copy-start = (bf16[2,528,2560]{2,1,0:T(8,128)(2,1)}, bf16[2,528,2560]{2,1,0:T(8,128)(2,1)S(1)}, u32[]{:S(2)}) copy-start(bf16[2,528,2560]{2,1,0:T(8,128)(2,1)S(1)} %get-tuple-element.16.table_ref) | copy-start | bytes 16220164
  34.2 3.9 %collective-permute-start = (bf16[128,16,128]{2,1,0:T(8,128)(2,1)S(1)}, bf16[128,16,128]{2,1,0:T(8,128)(2,1)S(1)}, u32[]{:S(2)}, u32[]{:S(2)}) collective-permute-start(bf16[128,16,128]{2,1,0:T(8,128)(2,1)S(1)} %all-to-all-done.own), channel_id=1, source_target_pairs={{0,1},{1,0},{2,3},{3,2},{4,5},{5,4},{6,7},{7,6},{8,9},{9,8},{10,11... | collective-permute-start | bytes 1572872 | tf_op jit(solution)/shard_map/ppermute | solution.py:398
